TPU v7x, 256 devices: a whole 4x4x8 slice. The times are simulated.
256 devices in a mesh: lat: 16 (over y, x_lo, core), lon: 16 (over z, x_hi).
Axes of the slice: x: 4 (x_hi: 2, x_lo: 2; x = x_hi * 2 + x_lo), y: 4, z: 8, core: 2. Of those that a mesh axis runs over, the one named last changes fastest.
Arguments:
- tokens: bfloat16 [2, 96, 192, 512], P(None, 'lat', 'lon'), may hold values from -6 to 6
- labels: int32 [2, 96, 192], P(None, 'lat', 'lon'), may hold values from 0 to 2
- gain_one: float32 [512], replicated, may hold values from 0.25 to 1.75
- project_one: bfloat16 [512, 1536], replicated, may hold values from -0.25 to 0.25
- output_one: bfloat16 [512, 512], replicated, may hold values from -0.25 to 0.25
- bias_one: bfloat16 [16, 144, 144], replicated, may hold values from -4 to 4
- gain_two: float32 [512], replicated, may hold values from 0.25 to 1.75
- project_two: bfloat16 [512, 1536], replicated, may hold values from -0.25 to 0.25
- output_two: bfloat16 [512, 512], replicated, may hold values from -0.25 to 0.25
- bias_two: bfloat16 [16, 144, 144], replicated, may hold values from -4 to 4
- gain_three: float32 [512], replicated, may hold values from 0.25 to 1.75
- up_weight: bfloat16 [512, 2048], replicated, may hold values from -0.25 to 0.25
- down_weight: bfloat16 [2048, 512], replicated, may hold values from -0.125 to 0.125
- cotangent: bfloat16 [2, 96, 192, 512], P(None, 'lat', 'lon'), may hold values from -6 to 6
Outputs:
- outputs: bfloat16 [2, 96, 192, 512], P(None, 'lat', 'lon')
- input_grad: bfloat16 [2, 96, 192, 512], P(None, 'lat', 'lon')
All inputs are finite; a program needn't handle non-finite values.
Results may differ from a plain program's by a relative error of at most 0.028.
Values may be sent and summed in bfloat16 or wider, within the bound.
A program may use at most 128 MiB of HBM per device.

v0:
```python
from functools import partial

import jax
import jax.numpy as jnp
from jax import lax
from jax.sharding import PartitionSpec as P

WLAT = 6
WLON = 12


EPSILON = 1e-05


def shifted_2(value, axis, steps):
    count = lax.axis_size(axis)
    pairs = [(source, (source + steps) % count) for source in range(count)]
    return lax.ppermute(value, axis, pairs)


def shortened(value):
    return jax.tree.map(lambda a: a.astype(jnp.bfloat16) if a.dtype == jnp.float32 else a, value)


def normalize(field_in, gain_vec):
    average = jnp.mean(field_in, axis=-1, keepdims=True)
    centred = field_in - average
    variance = jnp.mean(centred * centred, axis=-1, keepdims=True)
    return (centred * lax.rsqrt(variance + EPSILON) * gain_vec).astype(jnp.bfloat16)


def to_windows(grid_in, win_lat, win_lon):
    levels, lat_rows, lon_cols = (grid_in.shape[0], grid_in.shape[1], grid_in.shape[2])
    trailing = grid_in.shape[3:]
    parted = grid_in.reshape(
        (levels, lat_rows // win_lat, win_lat, lon_cols // win_lon, win_lon) + trailing
    )
    permute = (1, 3, 0, 2, 4) + tuple(range(5, 5 + len(trailing)))
    return parted.transpose(permute).reshape(
        (lat_rows // win_lat * (lon_cols // win_lon), levels * win_lat * win_lon) + trailing
    )


def from_windows(blocks, levels, lat_rows, lon_cols, win_lat, win_lon):
    trailing = blocks.shape[2:]
    parted = blocks.reshape(
        (lat_rows // win_lat, lon_cols // win_lon, levels, win_lat, win_lon) + trailing
    )
    permute = (2, 0, 3, 1, 4) + tuple(range(5, 5 + len(trailing)))
    return parted.transpose(permute).reshape((levels, lat_rows, lon_cols) + trailing)


def attend_heads(normed, allowed, bias_table, project):
    windows, tokens_win, features = normed.shape
    head_count = bias_table.shape[0]
    head_size = features // head_count
    packed = jnp.dot(normed, project, preferred_element_type=jnp.float32).astype(jnp.bfloat16)
    packed = packed.reshape(windows, tokens_win, 3, head_count, head_size)
    scores = jnp.einsum(
        "wqhd,wkhd->whqk", packed[:, :, 0], packed[:, :, 1], preferred_element_type=jnp.float32
    )
    scores = scores * head_size ** (-0.5) + bias_table.astype(jnp.float32)
    weights = jnp.exp(scores)
    if allowed is not None:
        weights = weights * allowed[:, None]
    probability = (weights / jnp.sum(weights, axis=-1, keepdims=True)).astype(jnp.bfloat16)
    heads_out = jnp.einsum(
        "whqk,wkhd->wqhd", probability, packed[:, :, 2], preferred_element_type=jnp.float32
    ).astype(jnp.bfloat16)
    return heads_out.reshape(windows, tokens_win, features)


def attend(normed, allowed, bias_table, project, output):
    heads_out = attend_heads(normed, allowed, bias_table, project)
    return jnp.dot(heads_out, output, preferred_element_type=jnp.float32)


def unshifted(field_in, gain_vec, bias_table, project, output):
    levels, lat_rows, lon_cols, features = field_in.shape
    normed = to_windows(normalize(field_in, gain_vec), WLAT, WLON)
    attended = attend(normed, None, bias_table, project, output)
    return field_in + from_windows(attended, levels, lat_rows, lon_cols, WLAT, WLON)


def shifted(field_in, group_ids, gain_vec, bias_table, project, output, win_lat):
    levels, lat_rows, lon_cols, features = field_in.shape
    normed = to_windows(normalize(field_in, gain_vec), win_lat, WLON)
    id_windows = to_windows(group_ids, win_lat, WLON)
    allowed = (id_windows[:, :, None] == id_windows[:, None, :]).astype(jnp.float32)
    attended = attend(normed, allowed, bias_table, project, output)
    return from_windows(attended, levels, lat_rows, lon_cols, win_lat, WLON)


def feed_forward(late_in, gain_vec, up_matrix, down_matrix):
    normed = normalize(late_in, gain_vec)
    hidden = jax.nn.gelu(
        jnp.dot(normed, up_matrix, preferred_element_type=jnp.float32), approximate=True
    ).astype(jnp.bfloat16)
    return late_in + jnp.dot(hidden, down_matrix, preferred_element_type=jnp.float32)


def roll_ahead(field_in, label_in):
    arrived = (
        shifted_2(field_in[:, :, : WLON // 2].astype(jnp.bfloat16), "lon", -1).astype(jnp.float32),
        shifted_2(label_in[:, :, : WLON // 2], "lon", -1),
    )
    field_lon = jnp.concatenate([field_in[:, :, WLON // 2 :], arrived[0]], axis=2)
    label_lon = jnp.concatenate([label_in[:, :, WLON // 2 :], arrived[1]], axis=2)
    arrived = shifted_2(
        (shortened(field_lon[:, : WLAT // 2]), label_lon[:, : WLAT // 2]), "lat", -1
    )
    main_field = jnp.concatenate([field_lon[:, WLAT // 2 :], arrived[0]], axis=1)
    main_label = jnp.concatenate([label_lon[:, WLAT // 2 :], arrived[1]], axis=1)
    return (main_field, main_label, field_lon[:, : WLAT // 2], label_lon[:, : WLAT // 2])


def roll_grad(field_in):
    arrived = shifted_2(shortened(field_in[:, :, : WLON // 2]), "lon", -1)
    field_lon = jnp.concatenate([field_in[:, :, WLON // 2 :], arrived], axis=2)
    arrived = shifted_2(shortened(field_lon[:, : WLAT // 2]), "lat", -1)
    return (
        jnp.concatenate([field_lon[:, WLAT // 2 :], arrived], axis=1),
        field_lon[:, : WLAT // 2],
    )


def roll_behind(main_field):
    arrived = shifted_2(shortened(main_field[:, -(WLAT // 2) :]), "lat", 1)
    field_lat = jnp.concatenate([arrived, main_field[:, : -(WLAT // 2)]], axis=1)
    arrived = shifted_2(shortened(field_lat[:, :, -(WLON // 2) :]), "lon", 1)
    return jnp.concatenate([arrived, field_lat[:, :, : -(WLON // 2)]], axis=2)


def per_device(
    tokens,
    labels,
    gain_one,
    project_one,
    output_one,
    bias_one,
    gain_two,
    project_two,
    output_two,
    bias_two,
    gain_three,
    up_weight,
    down_weight,
    cotangent,
):
    levels, lat_rows, lon_cols, features = tokens.shape
    half_lat = WLAT // 2
    head_count = bias_two.shape[0]
    last_row = lax.axis_index("lat") == lax.axis_size("lat") - 1
    row_index = jnp.arange(lat_rows, dtype=jnp.int32)
    pole_side = jnp.logical_and(last_row, row_index >= lat_rows - half_lat).astype(jnp.int32)
    first_fn = partial(
        unshifted, gain_vec=gain_one, bias_table=bias_one, project=project_one, output=output_one
    )
    middle, pull_first = jax.vjp(first_fn, tokens.astype(jnp.float32))
    pole_bias = bias_two.reshape(head_count, levels, WLAT, WLON, levels, WLAT, WLON)[
        :, :, half_lat:, :, :, half_lat:, :
    ]
    pole_bias = pole_bias.reshape(head_count, levels * half_lat * WLON, levels * half_lat * WLON)
    feed_part = partial(
        feed_forward, gain_vec=gain_three, up_matrix=up_weight, down_matrix=down_weight
    )
    main_field, main_label, pole_field, pole_label = roll_ahead(middle, labels)
    main_ids = main_label * 2 + pole_side[None, :, None]
    main_attend = partial(
        shifted,
        group_ids=main_ids,
        gain_vec=gain_two,
        bias_table=bias_two,
        project=project_two,
        output=output_two,
        win_lat=WLAT,
    )
    second_main, pull_main = jax.vjp(main_attend, main_field)
    late_sum = middle + roll_behind(second_main)
    result, pull_late = jax.vjp(feed_part, late_sum)
    grad_late = pull_late(cotangent.astype(jnp.float32))[0]
    seed_main, seed_pole = roll_grad(grad_late)
    back_main = pull_main(seed_main)[0]
    grad_middle = grad_late + roll_behind(back_main)
    gradient = pull_first(grad_middle)[0]
    return (result.astype(jnp.bfloat16), gradient.astype(jnp.bfloat16))


def solution(mesh):
    return jax.shard_map(
        per_device,
        mesh=mesh,
        in_specs=(
            P(None, "lat", "lon", None),
            P(None, "lat", "lon"),
            P(),
            P(),
            P(),
            P(),
            P(),
            P(),
            P(),
            P(),
            P(),
            P(),
            P(),
            P(None, "lat", "lon", None),
        ),
        out_specs=(P(None, "lat", "lon", None), P(None, "lat", "lon", None)),
        check_vma=False,
    )
```

profile of v0, /device:TPU:0, one launch (start us, length us, event | category | flops | bytes accessed | tf_op | source)
XLA Modules:
  0.0 149.6 jit_solution(6979125033254378602)
XLA Ops:
  1.6 6.6 %collective-permute-start.2 = (s32[2,6,6]{2,0,1:T(2,128)S(1)}, s32[2,6,6]{2,0,1:T(2,128)S(1)}, u32[]{:S(2)}, u32[]{:S(2)}) collective-permute-start(s32[2,6,6]{2,0,1:T(2,128)S(1)} %get-tuple-element.19), channel_id=1, source_target_pairs={{0,15},{1,0},{2,1},{3,2},{4,3},{5,4},{6,5},{7,6},{8,7},{9,8},{10,9... | collective-permute-start | bytes 872 | tf_op jit(solution)/shard_map/ppermute | solution.py:18
  8.2 1.8 %copy.43 = bf16[16,144,144]{1,2,0:T(8,128)(2,1)S(1)} copy(bf16[16,144,144]{2,1,0:T(8,128)(2,1)} %param.19) | data formatting | bytes 1327104 | tf_op args[5]
  12.8 2.7 %convolution_convert_fusion.2 = bf16[144,1536]{1,0:T(8,128)(2,1)} fusion(bf16[144,512]{1,0:T(8,128)(2,1)} %reshape.434, bf16[512,1536]{1,0:T(8,128)(2,1)} %param.17), kind=kOutput, calls=%fused_computation.7 | convolution fusion | flops 226713600 | bytes 2162688 | tf_op jit(solution)/shard_map/jvp()/dot_general | solution.py:57
  15.4 2.2 %copy.42 = bf16[144,1536]{0,1:T(8,128)(2,1)} copy(bf16[144,1536]{1,0:T(8,128)(2,1)} %convolution_convert_fusion.2) | data formatting | bytes 884736 | tf_op jit(solution)/shard_map/jvp()/convert_element_type | solution.py:57
  17.6 1.8 %fusion.142 = (f32[16,144]{1,0:T(8,128)S(1)}, f32[16,144,144]{1,2,0:T(8,128)S(1)}) fusion(bf16[16,144,144]{1,2,0:T(8,128)(2,1)S(1)} %copy.43, bf16[1,144,3,16,32]{1,4,3,2,0:T(8,128)(2,1)} %bitcast.161), kind=kOutput, calls=%fused_computation.205 | convolution fusion | flops 22558464 | bytes 2524160 | tf_op jit(solution)/shard_map/jvp(wqhd,wkhd->whqk)/dot_general | solution.py:59
  21.1 2.0 %fusion.62 = bf16[1,144,16,32]{1,3,2,0:T(8,128)(2,1)} fusion(bf16[16,144,144]{1,2,0:T(8,128)(2,1)S(1)} %divide_convert_fusion.1, bf16[1,144,3,16,32]{1,4,3,2,0:T(8,128)(2,1)} %bitcast.162), kind=kOutput, calls=%fused_computation.71 | convolution fusion | flops 21307392 | bytes 1073152 | tf_op jit(solution)/shard_map/jvp(whqk,wkhd->wqhd)/dot_general | solution.py:67
  23.0 2.2 %copy.45 = bf16[1,144,16,32]{3,2,1,0:T(8,128)(2,1)} copy(bf16[1,144,16,32]{1,3,2,0:T(8,128)(2,1)} %fusion.62) | data formatting | bytes 294912 | tf_op jit(solution)/shard_map/jvp()/convert_element_type | solution.py:69
  25.2 2.3 %dot_general.79 = bf16[2,6,12,512]{3,2,1,0:T(8,128)(2,1)} reshape(bf16[1,144,16,32]{3,2,1,0:T(8,128)(2,1)} %copy.45) | data formatting | bytes 294912 | tf_op jit(solution)/shard_map/jvp()/dot_general | solution.py:75
  30.9 2.8 %collective-permute-start.3 = (s32[2,3,12]{2,0,1:T(2,128)S(1)}, s32[2,3,12]{2,0,1:T(2,128)S(1)}, u32[]{:S(2)}, u32[]{:S(2)}) collective-permute-start(s32[2,3,12]{2,0,1:T(2,128)S(1)} %get-tuple-element.15), channel_id=1, source_target_pairs={{0,240},{16,0},{32,16},{48,32},{64,48},{80,64},{96,80},{112,96},{1... | collective-permute-start | bytes 872 | tf_op jit(solution)/shard_map/ppermute | solution.py:18
  35.5 2.6 %copy.47 = bf16[16,144,144]{1,2,0:T(8,128)(2,1)} copy(bf16[16,144,144]{2,1,0:T(8,128)(2,1)} %param.23) | data formatting | bytes 1327104 | tf_op args[9]
  47.8 2.7 %convolution_convert_fusion.1 = bf16[144,1536]{1,0:T(8,128)(2,1)} fusion(bf16[512,1536]{1,0:T(8,128)(2,1)} %param.21, f32[144,512]{1,0:T(8,128)} %concatenate.34, f32[512]{0:T(512)S(1)} %copy-done.28, f32[144]{0:T(256)S(1)} %rsqrt.35, f32[144]{0:T(256)S(1)} %div.116), kind=kOutput, calls=%fused_computation.6 | convolution fusion | flops 227008512 | bytes 2313344 | tf_op jit(solution)/shard_map/jvp()/dot_general | solution.py:57
  50.5 2.2 %copy.46 = bf16[144,1536]{0,1:T(8,128)(2,1)} copy(bf16[144,1536]{1,0:T(8,128)(2,1)} %convolution_convert_fusion.1) | data formatting | bytes 884736 | tf_op jit(solution)/shard_map/jvp()/convert_element_type | solution.py:57
  52.7 2.4 %multiply_reduce_fusion = (f32[16,144]{1,0:T(8,128)S(1)}, f32[16,144,144]{1,2,0:T(8,128)S(1)}) fusion(f32[144,144]{0,1:T(8,128)} %compare_convert_fusion, bf16[16,144,144]{1,2,0:T(8,128)(2,1)} %copy.47, bf16[1,144,3,16,32]{1,4,3,2,0:T(8,128)(2,1)} %bitcast.166), kind=kOutput, calls=%fused_computation.32 | convolution fusion | flops 22890240 | bytes 3187712 | tf_op jit(solution)/shard_map/jvp(wqhd,wkhd->whqk)/dot_general | solution.py:59
  57.8 2.0 %fusion.63 = bf16[1,144,16,32]{1,3,2,0:T(8,128)(2,1)} fusion(bf16[16,144,144]{1,2,0:T(8,128)(2,1)S(1)} %divide_convert_fusion, bf16[1,144,3,16,32]{1,4,3,2,0:T(8,128)(2,1)} %bitcast.167), kind=kOutput, calls=%fused_computation.72 | convolution fusion | flops 21307392 | bytes 1073152 | tf_op jit(solution)/shard_map/jvp(whqk,wkhd->wqhd)/dot_general | solution.py:67
  59.8 2.2 %copy.50 = bf16[1,144,16,32]{3,2,1,0:T(8,128)(2,1)} copy(bf16[1,144,16,32]{1,3,2,0:T(8,128)(2,1)} %fusion.63) | data formatting | bytes 294912 | tf_op jit(solution)/shard_map/jvp()/convert_element_type | solution.py:69
  62.0 2.3 %dot_general.84 = bf16[2,6,12,512]{3,2,1,0:T(8,128)(2,1)} reshape(bf16[1,144,16,32]{3,2,1,0:T(8,128)(2,1)} %copy.50) | data formatting | bytes 294912 | tf_op jit(solution)/shard_map/jvp()/dot_general | solution.py:75
  65.9 6.2 %collective-permute-done.4 = bf16[2,3,12,512]{3,2,1,0:T(8,128)(2,1)S(1)} collective-permute-done((bf16[2,3,12,512]{3,2,1,0:T(8,128)(2,1)S(1)}, bf16[2,3,12,512]{3,2,1,0:T(8,128)(2,1)S(1)}, u32[]{:S(2)}, u32[]{:S(2)}) %collective-permute-start.4) | collective-permute-done | bytes 73760 | tf_op jit(solution)/shard_map/ppermute | solution.py:18
  72.1 3.0 %collective-permute-start.5 = (bf16[2,6,6,512]{3,2,1,0:T(8,128)(2,1)S(1)}, bf16[2,6,6,512]{3,2,1,0:T(8,128)(2,1)S(1)}, u32[]{:S(2)}, u32[]{:S(2)}) collective-permute-start(bf16[2,6,6,512]{3,2,1,0:T(8,128)(2,1)S(1)} %fusion.106), channel_id=1, source_target_pairs={{0,1},{1,2},{2,3},{3,4},{4,5},{5,6},{6,7},{7,8},{8,9},{9,10},{10,1... | collective-permute-start | bytes 221192 | tf_op jit(solution)/shard_map/ppermute | solution.py:18
  75.1 5.5 %collective-permute-done.5 = bf16[2,6,6,512]{3,2,1,0:T(8,128)(2,1)S(1)} collective-permute-done((bf16[2,6,6,512]{3,2,1,0:T(8,128)(2,1)S(1)}, bf16[2,6,6,512]{3,2,1,0:T(8,128)(2,1)S(1)}, u32[]{:S(2)}, u32[]{:S(2)}) %collective-permute-start.5) | collective-permute-done | bytes 73760 | tf_op jit(solution)/shard_map/ppermute | solution.py:18
  81.6 1.8 %fusion.14 = f32[2,6,12,2048]{3,2,1,0:T(8,128)} fusion(bf16[512,2048]{1,0:T(8,128)(2,1)S(1)} %copy-done, f32[2,6,12,512]{3,2,1,0:T(8,128)S(1)} %get-tuple-element.7, f32[512]{0:T(512)S(1)} %copy-done.29, f32[2,6,12]{2,1,0:T(8,128)S(1)} %fusion.119, f32[2,6,12]{2,1,0:T(8,128)S(1)} %broadcast_multiply_fusion), kind=kOutput, calls=%fused_computation.27 | convolution fusion | flops 302284800 | bytes 3574912 | tf_op jit(solution)/shard_map/jvp()/dot_general | solution.py:97
  83.4 5.5 %multiply_reduce_fusion.1 = (f32[2,6,12]{2,1,0:T(8,128)}, f32[2,6,12,512]{3,2,1,0:T(8,128)}) fusion(f32[2,6,12,512]{3,2,1,0:T(8,128)} %copy-done.7, f32[2,6,12]{2,1,0:T(8,128)S(1)} %broadcast_multiply_fusion, f32[512]{0:T(512)S(1)} %copy-done.29, bf16[512,2048]{1,0:T(8,128)(2,1)S(1)} %copy-done, f32[2,6,12,2048]{3,2,1,0:T(8,128)} %fusion.14, ...), kind=kOutput, calls=%fused_computation.129 | convolution fusion | flops 610615168 | bytes 6114432 | tf_op jit(solution)/shard_map/transpose(jvp())/dot_general | solution.py:97
  94.3 5.1 %collective-permute-done.6 = bf16[2,6,6,512]{3,2,1,0:T(8,128)(2,1)S(1)} collective-permute-done((bf16[2,6,6,512]{3,2,1,0:T(8,128)(2,1)S(1)}, bf16[2,6,6,512]{3,2,1,0:T(8,128)(2,1)S(1)}, u32[]{:S(2)}, u32[]{:S(2)}) %collective-permute-start.6) | collective-permute-done | bytes 73760 | tf_op jit(solution)/shard_map/ppermute | solution.py:18
  99.5 2.2 %collective-permute-done.7 = bf16[2,3,12,512]{3,2,1,0:T(8,128)(2,1)S(1)} collective-permute-done((bf16[2,3,12,512]{3,2,1,0:T(8,128)(2,1)S(1)}, bf16[2,3,12,512]{3,2,1,0:T(8,128)(2,1)S(1)}, u32[]{:S(2)}, u32[]{:S(2)}) %collective-permute-start.7) | collective-permute-done | bytes 73760 | tf_op jit(solution)/shard_map/ppermute | solution.py:18
  104.1 2.1 %fusion.148 = bf16[144,512]{1,0:T(8,128)(2,1)} fusion(bf16[144,512]{1,0:T(8,128)(2,1)} %reshape.443, bf16[512,512]{1,0:T(8,128)(2,1)} %param.22), kind=kOutput, calls=%fused_computation.207 | convolution fusion | flops 75497472 | bytes 819200 | tf_op jit(solution)/shard_map/transpose(jvp())/dot_general | solution.py:75
  107.9 2.6 %fusion.6 = (f32[16,144]{1,0:T(8,128)S(1)}, bf16[16,144,144]{1,2,0:T(8,128)(2,1)S(1)}) fusion(f32[16,144,144]{1,2,0:T(8,128)} %copy-done.3, f32[16,144]{1,0:T(8,128)S(1)} %multiply_divide_fusion.1, f32[144,144]{0,1:T(8,128)} %compare_convert_fusion, bf16[16,32,144]{2,1,0:T(8,128)(2,1)} %bitcast.173, bf16[1,144,3,16,32]{1,4,3,2,0:T(8,128)(2,1)} %bitcast.168), kind=kOutput, calls=%fused_computation.13 | convolution fusion | flops 23222016 | bytes 3713024 | tf_op jit(solution)/shard_map/transpose(jvp(whqk,wkhd->wqhd))/dot_general | solution.py:67
  115.6 1.8 %reshape.451 = f32[2,6,12,512]{3,2,1,0:T(8,128)} reshape(f32[144,512]{1,0:T(8,128)} %get-tuple-element.29) | data formatting | bytes 589824 | tf_op jit(solution)/shard_map/transpose(jvp())/convert_element_type | solution.py:29
  120.4 6.2 %collective-permute-done.8 = bf16[2,3,12,512]{3,2,1,0:T(8,128)(2,1)S(1)} collective-permute-done((bf16[2,3,12,512]{3,2,1,0:T(8,128)(2,1)S(1)}, bf16[2,3,12,512]{3,2,1,0:T(8,128)(2,1)S(1)}, u32[]{:S(2)}, u32[]{:S(2)}) %collective-permute-start.8) | collective-permute-done | bytes 73760 | tf_op jit(solution)/shard_map/ppermute | solution.py:18
  126.7 1.8 %collective-permute-start.9 = (bf16[2,6,6,512]{3,2,1,0:T(8,128)(2,1)S(1)}, bf16[2,6,6,512]{3,2,1,0:T(8,128)(2,1)S(1)}, u32[]{:S(2)}, u32[]{:S(2)}) collective-permute-start(bf16[2,6,6,512]{3,2,1,0:T(8,128)(2,1)S(1)} %fusion.103), channel_id=1, source_target_pairs={{0,1},{1,2},{2,3},{3,4},{4,5},{5,6},{6,7},{7,8},{8,9},{9,10},{10,1... | collective-permute-start | bytes 221192 | tf_op jit(solution)/shard_map/ppermute | solution.py:18
  128.5 2.3 %fusion.55 = bf16[2,6,12,512]{3,2,1,0:T(8,128)(2,1)S(1)} fusion(f32[2,6,12,512]{3,2,1,0:T(8,128)S(1)} %copy-done.8, bf16[2048,512]{1,0:T(8,128)(2,1)} %param.26, f32[2,6,12,2048]{3,2,1,0:T(8,128)S(1)} %copy-done.26), kind=kOutput, calls=%fused_computation.66 | convolution fusion | flops 304791552 | bytes 3719168 | tf_op jit(solution)/shard_map/jvp()/dot_general | solution.py:99
  131.6 3.6 %collective-permute-done.9 = bf16[2,6,6,512]{3,2,1,0:T(8,128)(2,1)S(1)} collective-permute-done((bf16[2,6,6,512]{3,2,1,0:T(8,128)(2,1)S(1)}, bf16[2,6,6,512]{3,2,1,0:T(8,128)(2,1)S(1)}, u32[]{:S(2)}, u32[]{:S(2)}) %collective-permute-start.9) | collective-permute-done | bytes 73760 | tf_op jit(solution)/shard_map/ppermute | solution.py:18
  137.8 2.1 %fusion.147 = bf16[144,512]{1,0:T(8,128)(2,1)} fusion(bf16[144,512]{1,0:T(8,128)(2,1)} %reshape.447, bf16[512,512]{1,0:T(8,128)(2,1)} %param.18), kind=kOutput, calls=%fused_computation.206 | convolution fusion | flops 75497472 | bytes 819200 | tf_op jit(solution)/shard_map/transpose(jvp())/dot_general | solution.py:75
  141.6 2.6 %fusion.11 = (f32[16,144]{1,0:T(8,128)S(1)}, bf16[16,144,144]{1,2,0:T(8,128)(2,1)S(1)}) fusion(f32[16,144,144]{1,2,0:T(8,128)} %copy-done.1, f32[16,144]{1,0:T(8,128)S(1)} %multiply_divide_fusion, bf16[16,32,144]{2,1,0:T(8,128)(2,1)} %bitcast.175, bf16[1,144,3,16,32]{1,4,3,2,0:T(8,128)(2,1)} %bitcast.163), kind=kOutput, calls=%fused_computation.18 | convolution fusion | flops 22890240 | bytes 3565568 | tf_op jit(solution)/shard_map/transpose(jvp(whqk,wkhd->wqhd))/dot_general | solution.py:67
  (156 shorter events, 53.3 us)
Async XLA Ops:
  0.6 80.9 %copy-start = (bf16[512,2048]{1,0:T(8,128)(2,1)S(1)}, bf16[512,2048]{1,0:T(8,128)(2,1)}, u32[]{:S(2)}) copy-start(bf16[512,2048]{1,0:T(8,128)(2,1)} %param.25) | copy-start | bytes 6291460
  0.6 9.3 %copy-start.9 = (bf16[2,6,12,512]{3,0,2,1:T(2,128)(2,1)S(1)}, bf16[2,6,12,512]{3,0,2,1:T(2,128)(2,1)}, u32[]{:S(2)}) copy-start(bf16[2,6,12,512]{3,0,2,1:T(2,128)(2,1)} %param.14) | copy-start | bytes 442372
  0.7 9.7 %copy-start.27 = (f32[512]{0:T(512)S(1)}, f32[512]{0:T(512)}, u32[]{:S(2)}) copy-start(f32[512]{0:T(512)} %param.16) | copy-start | bytes 6148
  1.6 29.3 %collective-permute-start.2 = (s32[2,6,6]{2,0,1:T(2,128)S(1)}, s32[2,6,6]{2,0,1:T(2,128)S(1)}, u32[]{:S(2)}, u32[]{:S(2)}) collective-permute-start(s32[2,6,6]{2,0,1:T(2,128)S(1)} %get-tuple-element.19), channel_id=1, source_target_pairs={{0,15},{1,0},{2,1},{3,2},{4,3},{5,4},{6,5},{7,6},{8,7},{9,8},{10,9... | collective-permute-start | bytes 872 | tf_op jit(solution)/shard_map/ppermute | solution.py:18
  19.4 1.4 copy-start.1
  30.3 8.6 %collective-permute-start = (bf16[2,6,6,512]{3,2,1,0:T(8,128)(2,1)}, bf16[2,6,6,512]{3,2,1,0:T(8,128)(2,1)}, u32[]{:S(2)}, u32[]{:S(2)}) collective-permute-start(bf16[2,6,6,512]{3,2,1,0:T(8,128)(2,1)} %slice.195), channel_id=1, source_target_pairs={{0,15},{1,0},{2,1},{3,2},{4,3},{5,4},{6,5},{7,6},{8,7},{9,8},{10,9... | collective-permute-start | bytes 221192 | tf_op jit(solution)/shard_map/ppermute | solution.py:18
  30.9 7.1 %collective-permute-start.3 = (s32[2,3,12]{2,0,1:T(2,128)S(1)}, s32[2,3,12]{2,0,1:T(2,128)S(1)}, u32[]{:S(2)}, u32[]{:S(2)}) collective-permute-start(s32[2,3,12]{2,0,1:T(2,128)S(1)} %get-tuple-element.15), channel_id=1, source_target_pairs={{0,240},{16,0},{32,16},{48,32},{64,48},{80,64},{96,80},{112,96},{1... | collective-permute-start | bytes 872 | tf_op jit(solution)/shard_map/ppermute | solution.py:18
  38.0 9.7 %copy-start.28 = (f32[512]{0:T(512)S(1)}, f32[512]{0:T(512)}, u32[]{:S(2)}) copy-start(f32[512]{0:T(512)} %param.20) | copy-start | bytes 6148
  40.8 3.5 %collective-permute-start.1 = (bf16[2,3,12,512]{3,2,1,0:T(8,128)(2,1)S(1)}, bf16[2,3,12,512]{3,2,1,0:T(8,128)(2,1)S(1)}, u32[]{:S(2)}, u32[]{:S(2)}) collective-permute-start(bf16[2,3,12,512]{3,2,1,0:T(8,128)(2,1)S(1)} %fusion.109), channel_id=1, source_target_pairs={{0,240},{16,0},{32,16},{48,32},{64,48},{80,64},{96,80},{112,96},{1... | collective-permute-start | bytes 221192 | tf_op jit(solution)/shard_map/ppermute | solution.py:18
  43.1 1.4 copy-start.16
  52.7 3.8 %copy-start.22 = (f32[144,144]{0,1:T(8,128)S(1)}, f32[144,144]{0,1:T(8,128)}, u32[]{:S(2)}) copy-start(f32[144,144]{0,1:T(8,128)} %compare_convert_fusion) | copy-start | bytes 248836
  55.1 1.4 copy-start.3
  64.3 16.4 %copy-start.19 = (f32[2,6,12,512]{3,2,1,0:T(8,128)S(1)}, f32[2,6,12,512]{3,2,1,0:T(8,128)}, u32[]{:S(2)}) copy-start(f32[2,6,12,512]{3,2,1,0:T(8,128)} %copy-done.18) | copy-start | bytes 884740
  64.3 17.3 %copy-start.29 = (f32[512]{0:T(512)S(1)}, f32[512]{0:T(512)}, u32[]{:S(2)}) copy-start(f32[512]{0:T(512)} %param.24) | copy-start | bytes 6148
  65.7 6.3 %collective-permute-start.4 = (bf16[2,3,12,512]{3,2,1,0:T(8,128)(2,1)S(1)}, bf16[2,3,12,512]{3,2,1,0:T(8,128)(2,1)S(1)}, u32[]{:S(2)}, u32[]{:S(2)}) collective-permute-start(bf16[2,3,12,512]{3,2,1,0:T(8,128)(2,1)S(1)} %slice.194), channel_id=1, source_target_pairs={{0,16},{16,32},{32,48},{48,64},{64,80},{80,96},{96,112},{112,128},... | collective-permute-start | bytes 221192 | tf_op jit(solution)/shard_map/ppermute | solution.py:18
  72.1 8.5 %collective-permute-start.5 = (bf16[2,6,6,512]{3,2,1,0:T(8,128)(2,1)S(1)}, bf16[2,6,6,512]{3,2,1,0:T(8,128)(2,1)S(1)}, u32[]{:S(2)}, u32[]{:S(2)}) collective-permute-start(bf16[2,6,6,512]{3,2,1,0:T(8,128)(2,1)S(1)} %fusion.106), channel_id=1, source_target_pairs={{0,1},{1,2},{2,3},{3,4},{4,5},{5,6},{6,7},{7,8},{8,9},{9,10},{10,1... | collective-permute-start | bytes 221192 | tf_op jit(solution)/shard_map/ppermute | solution.py:18
  93.2 6.2 %collective-permute-start.6 = (bf16[2,6,6,512]{3,2,1,0:T(8,128)(2,1)S(1)}, bf16[2,6,6,512]{3,2,1,0:T(8,128)(2,1)S(1)}, u32[]{:S(2)}, u32[]{:S(2)}) collective-permute-start(bf16[2,6,6,512]{3,2,1,0:T(8,128)(2,1)S(1)} %get-tuple-element.9), channel_id=1, source_target_pairs={{0,15},{1,0},{2,1},{3,2},{4,3},{5,4},{6,5},{7,6},{8,7},{9,8},{10,9... | collective-permute-start | bytes 221192 | tf_op jit(solution)/shard_map/ppermute | solution.py:18
  99.4 2.3 %collective-permute-start.7 = (bf16[2,3,12,512]{3,2,1,0:T(8,128)(2,1)S(1)}, bf16[2,3,12,512]{3,2,1,0:T(8,128)(2,1)S(1)}, u32[]{:S(2)}, u32[]{:S(2)}) collective-permute-start(bf16[2,3,12,512]{3,2,1,0:T(8,128)(2,1)S(1)} %get-tuple-element.13), channel_id=1, source_target_pairs={{0,240},{16,0},{32,16},{48,32},{64,48},{80,64},{96,80},{112,96},{1... | collective-permute-start | bytes 221192 | tf_op jit(solution)/shard_map/ppermute | solution.py:18
  107.9 2.7 %copy-start.4 = (f32[16,144,144]{1,2,0:T(8,128)S(1)}, f32[16,144,144]{1,2,0:T(8,128)}, u32[]{:S(2)}) copy-start(f32[16,144,144]{1,2,0:T(8,128)} %copy-done.3) | copy-start | bytes 3981316
  107.9 2.8 %copy-start.14 = (bf16[144,1536]{0,1:T(8,128)(2,1)S(1)}, bf16[144,1536]{0,1:T(8,128)(2,1)}, u32[]{:S(2)}) copy-start(bf16[144,1536]{0,1:T(8,128)(2,1)} %copy.46) | copy-start | bytes 1327108
  107.9 2.8 %copy-start.23 = (f32[144,144]{0,1:T(8,128)S(1)}, f32[144,144]{0,1:T(8,128)}, u32[]{:S(2)}) copy-start(f32[144,144]{0,1:T(8,128)} %compare_convert_fusion) | copy-start | bytes 248836
  111.4 1.3 copy-start.24
  112.7 1.4 copy-start.10
  112.7 1.4 copy-start.12
  118.8 9.7 %copy-start.8 = (f32[2,6,12,512]{3,2,1,0:T(8,128)S(1)}, f32[2,6,12,512]{3,2,1,0:T(8,128)}, u32[]{:S(2)}) copy-start(f32[2,6,12,512]{3,2,1,0:T(8,128)} %copy-done.7) | copy-start | bytes 884740
  118.8 9.7 %copy-start.26 = (f32[2,6,12,2048]{3,2,1,0:T(8,128)S(1)}, f32[2,6,12,2048]{3,2,1,0:T(8,128)}, u32[]{:S(2)}) copy-start(f32[2,6,12,2048]{3,2,1,0:T(8,128)} %fusion.14) | copy-start | bytes 3538948
  120.3 6.3 %collective-permute-start.8 = (bf16[2,3,12,512]{3,2,1,0:T(8,128)(2,1)S(1)}, bf16[2,3,12,512]{3,2,1,0:T(8,128)(2,1)S(1)}, u32[]{:S(2)}, u32[]{:S(2)}) collective-permute-start(bf16[2,3,12,512]{3,2,1,0:T(8,128)(2,1)S(1)} %slice.192), channel_id=1, source_target_pairs={{0,16},{16,32},{32,48},{48,64},{64,80},{80,96},{96,112},{112,128},... | collective-permute-start | bytes 221192 | tf_op jit(solution)/shard_map/ppermute | solution.py:18
  126.7 8.6 %copy-start.21 = (f32[2,6,12,512]{3,2,1,0:T(8,128)S(1)}, f32[2,6,12,512]{3,2,1,0:T(8,128)}, u32[]{:S(2)}) copy-start(f32[2,6,12,512]{3,2,1,0:T(8,128)} %copy-done.20) | copy-start | bytes 884740
  126.7 8.5 %collective-permute-start.9 = (bf16[2,6,6,512]{3,2,1,0:T(8,128)(2,1)S(1)}, bf16[2,6,6,512]{3,2,1,0:T(8,128)(2,1)S(1)}, u32[]{:S(2)}, u32[]{:S(2)}) collective-permute-start(bf16[2,6,6,512]{3,2,1,0:T(8,128)(2,1)S(1)} %fusion.103), channel_id=1, source_target_pairs={{0,1},{1,2},{2,3},{3,4},{4,5},{5,6},{6,7},{7,8},{8,9},{9,10},{10,1... | collective-permute-start | bytes 221192 | tf_op jit(solution)/shard_map/ppermute | solution.py:18
  141.6 2.6 %copy-start.2 = (f32[16,144,144]{1,2,0:T(8,128)S(1)}, f32[16,144,144]{1,2,0:T(8,128)}, u32[]{:S(2)}) copy-start(f32[16,144,144]{1,2,0:T(8,128)} %copy-done.1) | copy-start | bytes 3981316
  141.6 2.7 %copy-start.13 = (bf16[144,1536]{0,1:T(8,128)(2,1)S(1)}, bf16[144,1536]{0,1:T(8,128)(2,1)}, u32[]{:S(2)}) copy-start(bf16[144,1536]{0,1:T(8,128)(2,1)} %copy.42) | copy-start | bytes 1327108
  145.9 1.4 copy-start.11
  (8 other events, 7.5 us)
where the time goes:
time: 151 us; the launch traced here: 150 us
  local copies, waits for them, and re-layouts  44.2 us (29%)
  matrix products  40.9 us (27%)
  waiting for transfers between devices  30 us (20%)
  starting transfers between devices  17.4 us (12%)
  other arithmetic  15.6 us (10%)
    ppermute x10, waiting for transfers between devices, shifted_2(): return lax.ppermute(value, axis, pairs)  30 us
    ppermute x10, starting transfers between devices, shifted_2(): return lax.ppermute(value, axis, pairs)  17.4 us
    unnamed x64, local copies, waits for them, and re-layouts  15.1 us
    dot_general x6, matrix products, attend_heads(): jnp.einsum('whqk,wkhd->wqhd', probability, packed[:, :, 2], preferred_ele...  10.1 us
    dot_general x4, matrix products, attend_heads(): jnp.dot(normed, project, preferred_element_type=jnp.float32)  7.43 us
    dot_general x2, matrix products, feed_forward(): jnp.dot(normed, up_matrix, preferred_element_type=jnp.float32)  7.33 us
    dot_general x4, matrix products, attend(): return jnp.dot(heads_out, output, preferred_element_type=jnp.float32)  7.06 us
    dot_general x6, matrix products, attend_heads(): jnp.einsum('wqhd,wkhd->whqk', packed[:, :, 0], packed[:, :, 1], preferred...  6.79 us
  transfers between devices with their start and end apart: 10, of which 7 were waited for; matrix products, arithmetic and copies ran while one was open for 20% of the time, Pallas kernels for 0%

commit v1 on v0

v1 whole, which is shorter than its diff:
```python
import functools

import jax
import jax.numpy as jnp
import numpy as np
from jax import lax
from jax.experimental import pallas as pl
from jax.experimental.pallas import tpu as pltpu
from jax.sharding import PartitionSpec as P

MESH = pl.DeviceIdType.MESH
BF = jnp.bfloat16
F32 = jnp.float32

WLAT = 6
WLON = 12
LEV = 2
WT = LEV * WLAT * WLON
QUAD = WT // 4
SLOT = 48
ROWS = 4 * SLOT
D = 512
FF = 2048
HEADS = 16
HD = D // HEADS
LANES = 128
PER = LANES // HD
GROUPS = D // LANES
SCALE = HD ** (-0.5)
EPSILON = 1e-05


def quadrant_matrix():
    place = np.zeros((ROWS, WT), np.float32)
    hl, hc = WLAT // 2, WLON // 2
    for half_row in range(2):
        for half_col in range(2):
            for i in range(QUAD):
                level, r, c = i // (hl * hc), i // hc % hl, i % hc
                token = level * WLAT * WLON + (half_row * hl + r) * WLON + half_col * hc + c
                place[SLOT * (2 * half_row + half_col) + i, token] = 1.0
    return place


def nn(a, b):
    return lax.dot_general(a, b, (((1,), (0,)), ((), ())), preferred_element_type=F32)


def nt(a, b):
    return lax.dot_general(a, b, (((1,), (1,)), ((), ())), preferred_element_type=F32)


def tn(a, b):
    return lax.dot_general(a, b, (((0,), (0,)), ((), ())), preferred_element_type=F32)


def norm_parts(x):
    centred = x - jnp.mean(x, axis=-1, keepdims=True)
    rs = lax.rsqrt(jnp.mean(centred * centred, axis=-1, keepdims=True) + EPSILON)
    return centred * rs, rs


def norm_back(hat, rs, gain, dy):
    t = dy * gain
    return rs * (
        t - jnp.mean(t, axis=-1, keepdims=True) - hat * jnp.mean(t * hat, axis=-1, keepdims=True)
    )


def head_masks():
    lane = lax.broadcasted_iota(jnp.int32, (WT, LANES), 1)
    return [jnp.logical_and(lane >= HD * j, lane < HD * (j + 1)) for j in range(PER)]


def pick(stack, masks):
    out = stack[:WT]
    for j in range(1, PER):
        out = jnp.where(masks[j], stack[WT * j : WT * (j + 1)], out)
    return out


def spread(group, masks):
    zero = jnp.zeros_like(group)
    return jnp.concatenate([jnp.where(m, group, zero) for m in masks], axis=0)


def attention(packed, bias, probs, heads, allowed, masks):
    for g in range(GROUPS):
        lanes = slice(LANES * g, LANES * (g + 1))
        q = packed[:, LANES * g : LANES * (g + 1)]
        k = packed[:, D + LANES * g : D + LANES * (g + 1)]
        v = packed[:, 2 * D + LANES * g : 2 * D + LANES * (g + 1)]
        s = nt(spread(q, masks), k)
        for j in range(PER):
            h = PER * g + j
            e = jnp.exp(s[WT * j : WT * (j + 1)] * SCALE + bias[h].astype(F32))
            if allowed is not None:
                e = e * allowed
            z = jnp.sum(e, axis=-1, keepdims=True)
            down = jnp.where(z > 2.0**64, 2.0**-64, 1.0).astype(F32)
            probs[pl.ds(WT * h, WT), :] = ((e * down) * (1.0 / (z * down))).astype(BF)
        o = nn(probs[pl.ds(WT * PER * g, WT * PER), :], v)
        heads[:, lanes] = pick(o, masks).astype(BF)


def attention_back(packed, probs, heads, d_heads, d_packed, masks):
    for g in range(GROUPS):
        q = packed[:, LANES * g : LANES * (g + 1)]
        k = packed[:, D + LANES * g : D + LANES * (g + 1)]
        v = packed[:, 2 * D + LANES * g : 2 * D + LANES * (g + 1)]
        do = d_heads[:, LANES * g : LANES * (g + 1)]
        o = heads[:, LANES * g : LANES * (g + 1)]
        less = (-(do.astype(F32) * o.astype(F32))).astype(BF)
        do_stack = spread(do, masks)
        left = jnp.concatenate([do_stack, spread(less, masks)], axis=1)
        right = jnp.concatenate([v, jnp.ones_like(v)], axis=1)
        dp = nt(left, right)
        p = probs[pl.ds(WT * PER * g, WT * PER), :]
        ds = (p.astype(F32) * dp).astype(BF)
        dq = pick(nn(ds, k), masks) * SCALE
        dk = tn(ds, spread(q, masks)) * SCALE
        dv = tn(p, do_stack)
        d_packed[:, LANES * g : LANES * (g + 1)] = dq.astype(BF)
        d_packed[:, D + LANES * g : D + LANES * (g + 1)] = dk.astype(BF)
        d_packed[:, 2 * D + LANES * g : 2 * D + LANES * (g + 1)] = dv.astype(BF)


def kernel(
    n_lat, n_lon,
    tokens, labels, gain_one, project_one, output_one, bias_one, gain_two, project_two, output_two,
    bias_two, gain_three, up_weight, down_weight, cotangent, to_quad, from_quad,
    outputs, input_grad,
    tok, lab, g1, w1, wo1, b1, g2, w2, wo2, b2, g3, wup, wdn, cot, tq, fq,
    x, ct, packed_one, packed_two, probs_one, probs_two, heads_one, heads_two, d_heads, d_packed,
    middle, hat_one, hat_two, u_keep, dh_keep, result, allowed_ref,
    out_stage, grad_stage,
    send, recv, lab_send, lab_recv,
    load_sem, send_sem, recv_sem, lab_send_sem, lab_recv_sem, out_sem,
):
    i = lax.axis_index("lat")
    j = lax.axis_index("lon")
    north, south = lax.rem(i + n_lat - 1, n_lat), lax.rem(i + 1, n_lat)
    west, east = lax.rem(j + n_lon - 1, n_lon), lax.rem(j + 1, n_lon)
    barrier = pltpu.get_barrier_semaphore()
    around = [(i, east), (south, j), (south, east), (i, west), (north, j), (north, west)]
    for device in around:
        pl.semaphore_signal(barrier, inc=1, device_id=device, device_id_type=MESH)

    pairs = {
        "tok": (tokens, tok), "g1": (gain_one, g1), "w1": (project_one, w1), "b1": (bias_one, b1),
        "lab": (labels, lab), "tq": (to_quad, tq), "fq": (from_quad, fq),
        "wo1": (output_one, wo1), "g2": (gain_two, g2), "cot": (cotangent, cot), "w2": (project_two, w2),
        "wdn": (down_weight, wdn), "b2": (bias_two, b2),
        "wo2": (output_two, wo2), "g3": (gain_three, g3), "wup": (up_weight, wup),
    }
    loads = {}
    for at, (name, (source, target)) in enumerate(pairs.items()):
        loads[name] = pltpu.make_async_copy(source, target, load_sem.at[at])
        loads[name].start()

    masks = head_masks()

    def to_rows(source, target):
        for a in range(LEV):
            for b in range(WLAT):
                target[pl.ds((a * WLAT + b) * WLON, WLON), :] = source[a, b].astype(F32)

    owner_target = {0: (north, west), 1: (north, j), 2: (i, west)}
    window_target = {3: (south, east), 2: (south, j), 1: (i, east)}

    def exchange(step, targets):
        copies = []
        for q, device in targets.items():
            copies.append(
                pltpu.make_async_remote_copy(
                    src_ref=send.at[step, pl.ds(SLOT * q, SLOT)],
                    dst_ref=recv.at[step, pl.ds(SLOT * (3 - q), SLOT)],
                    send_sem=send_sem.at[step, q],
                    recv_sem=recv_sem.at[step, q],
                    device_id=device,
                    device_id_type=MESH,
                )
            )
        return copies

    def start(step, targets, value):
        rows = nn(tq[...], value).astype(BF)
        send[step] = rows
        stay = 3 if step % 2 == 0 else 0
        recv[step, pl.ds(SLOT * (3 - stay), SLOT)] = rows[SLOT * stay : SLOT * (stay + 1)]
        copies = exchange(step, targets)
        for copy in copies:
            copy.start()
        return copies

    def arrived(step, copies):
        for copy in copies:
            copy.wait_recv()
        return nn(fq[...], recv[step]).astype(BF)

    loads["tok"].wait()
    to_rows(tok, x)
    loads["g1"].wait()
    hat, rs_one = norm_parts(x[...])
    hat_one[...] = hat
    normed = (hat * g1[...]).astype(BF)
    loads["w1"].wait()
    packed_one[...] = nn(normed, w1[...]).astype(BF)

    loads["lab"].wait()
    loads["tq"].wait()
    loads["fq"].wait()
    token = lax.broadcasted_iota(jnp.int32, (WT, WLON), 0)
    column = lax.broadcasted_iota(jnp.int32, (WT, WLON), 1)
    labelled = jnp.zeros((WT, WLON), F32)
    for a in range(LEV):
        level = lab[a].astype(F32)
        for b in range(WLAT):
            line = jnp.broadcast_to(level[b : b + 1, :], (WT, WLON))
            labelled = jnp.where(token - (a * WLAT + b) * WLON == column, line, labelled)
    label_col = jnp.sum(labelled, axis=-1, keepdims=True)
    label_rows = nn(tq[...], jnp.broadcast_to(label_col, (WT, LANES)).astype(BF)).astype(BF)
    lab_send[...] = label_rows
    lab_recv[pl.ds(0, SLOT)] = label_rows[3 * SLOT :]
    pl.semaphore_wait(barrier, len(around))
    lab_copies = []
    for q, device in owner_target.items():
        lab_copies.append(
            pltpu.make_async_remote_copy(
                src_ref=lab_send.at[pl.ds(SLOT * q, SLOT)],
                dst_ref=lab_recv.at[pl.ds(SLOT * (3 - q), SLOT)],
                send_sem=lab_send_sem.at[q],
                recv_sem=lab_recv_sem.at[q],
                device_id=device,
                device_id_type=MESH,
            )
        )
        lab_copies[-1].start()

    loads["b1"].wait()
    attention(packed_one, b1, probs_one, heads_one, None, masks)
    loads["wo1"].wait()
    mid = x[...] + nn(heads_one[...], wo1[...])
    middle[...] = mid
    hat, rs_two = norm_parts(mid)
    hat_two[...] = hat
    loads["g2"].wait()
    copies_0 = start(0, owner_target, (hat * g2[...]).astype(BF))

    loads["cot"].wait()
    to_rows(cot, ct)
    loads["wdn"].wait()
    dh_keep[...] = nt(ct[...].astype(BF), wdn[...]).astype(BF)
    for copy in lab_copies:
        copy.wait_recv()
    label_here = nn(fq[...], lab_recv[...])
    row = lax.broadcasted_iota(jnp.int32, (WT, LANES), 0)
    half = WLAT * WLON
    late_row = jnp.logical_or(
        jnp.logical_and(row >= half // 2, row < half), row >= half + half // 2
    )
    edge = jnp.where(i == n_lat - 1, 1.0, 0.0).astype(F32)
    ids = label_here * 2.0 + jnp.where(late_row, edge, 0.0)
    lane = lax.broadcasted_iota(jnp.int32, (WT, LANES), 1).astype(F32)
    one_hot = jnp.where(ids == lane, 1.0, 0.0).astype(BF)
    allowed_ref[...] = nt(one_hot, one_hot)

    loads["w2"].wait()
    loads["b2"].wait()
    normed = arrived(0, copies_0)

    packed_two[...] = nn(normed, w2[...]).astype(BF)
    attention(packed_two, b2, probs_two, heads_two, allowed_ref[...], masks)
    copies_1 = start(1, window_target, heads_two[...])
    loads["wo2"].wait()
    loads["g3"].wait()
    loads["wup"].wait()
    late = middle[...] + nn(arrived(1, copies_1), wo2[...])

    hat, rs_three = norm_parts(late)
    u = nn((hat * g3[...]).astype(BF), wup[...])
    root = (2.0 / np.pi) ** 0.5
    square = u * u
    bent = jnp.tanh(root * u * (1.0 + 0.044715 * square))
    slope = 0.5 * (1.0 + bent) + (0.5 * root) * u * (1.0 - bent * bent) * (
        1.0 + (3.0 * 0.044715) * square
    )
    du = (dh_keep[...].astype(F32) * slope).astype(BF)
    hidden = (0.5 * u * (1.0 + bent)).astype(BF)
    u_keep[...] = hidden
    dn = nt(du, wup[...]).astype(BF).astype(F32)
    d_late = ct[...] + norm_back(hat, rs_three, g3[...], dn)
    copies_2 = start(2, owner_target, nt(d_late.astype(BF), wo2[...]).astype(BF))

    result[...] = late + nn(u_keep[...], wdn[...])
    for a in range(LEV):
        for b in range(WLAT):
            out_stage[a, b] = result[pl.ds((a * WLAT + b) * WLON, WLON), :].astype(BF)
    out_copy = pltpu.make_async_copy(out_stage, outputs, out_sem.at[0])
    out_copy.start()

    d_heads[...] = arrived(2, copies_2)
    attention_back(packed_two, probs_two, heads_two, d_heads, d_packed, masks)
    copies_3 = start(3, window_target, nt(d_packed[...], w2[...]).astype(BF))
    dn = arrived(3, copies_3).astype(F32)
    d_mid = d_late + norm_back(hat_two[...], rs_two, g2[...], dn)

    d_heads[...] = nt(d_mid.astype(BF), wo1[...]).astype(BF)
    attention_back(packed_one, probs_one, heads_one, d_heads, d_packed, masks)
    dn = nt(d_packed[...], w1[...]).astype(BF).astype(F32)
    result[...] = d_mid + norm_back(hat_one[...], rs_one, g1[...], dn)
    for a in range(LEV):
        for b in range(WLAT):
            grad_stage[a, b] = result[pl.ds((a * WLAT + b) * WLON, WLON), :].astype(BF)
    grad_copy = pltpu.make_async_copy(grad_stage, input_grad, out_sem.at[1])
    grad_copy.start()
    for copy in lab_copies + copies_0 + copies_1 + copies_2 + copies_3:
        copy.wait_send()
    out_copy.wait()
    grad_copy.wait()


def per_device(n_lat, n_lon, *args):
    (tokens, labels, g1, w1, wo1, b1, g2, w2, wo2, b2, g3, wup, wdn, cot) = args
    place = quadrant_matrix()
    to_quad = jnp.asarray(place, BF)
    from_quad = jnp.asarray(place.T, BF)
    operands = (
        tokens, labels, g1.reshape(1, D), w1, wo1, b1, g2.reshape(1, D), w2, wo2, b2,
        g3.reshape(1, D), wup, wdn, cot, to_quad, from_quad,
    )
    vm = pltpu.VMEM
    landing = [vm(a.shape, a.dtype) for a in operands]
    block = tokens.shape
    scratch = landing + [
        vm((WT, D), F32), vm((WT, D), F32),
        vm((WT, 3 * D), BF), vm((WT, 3 * D), BF),
        vm((HEADS * WT, WT), BF), vm((HEADS * WT, WT), BF),
        vm((WT, D), BF), vm((WT, D), BF), vm((WT, D), BF), vm((WT, 3 * D), BF),
        vm((WT, D), F32), vm((WT, D), F32), vm((WT, D), F32),
        vm((WT, FF), BF), vm((WT, FF), BF), vm((WT, D), F32), vm((WT, WT), F32),
        vm(block, BF), vm(block, BF),
        vm((4, ROWS, D), BF), vm((4, ROWS, D), BF), vm((ROWS, LANES), BF), vm((ROWS, LANES), BF),
        pltpu.SemaphoreType.DMA((len(operands),)),
        pltpu.SemaphoreType.DMA((4, 4)), pltpu.SemaphoreType.DMA((4, 4)),
        pltpu.SemaphoreType.DMA((4,)), pltpu.SemaphoreType.DMA((4,)),
        pltpu.SemaphoreType.DMA((2,)),
    ]
    whole = pl.BlockSpec(memory_space=pl.ANY)
    return pl.pallas_call(
        functools.partial(kernel, n_lat, n_lon),
        out_shape=(jax.ShapeDtypeStruct(block, BF), jax.ShapeDtypeStruct(block, BF)),
        in_specs=[whole] * len(operands),
        out_specs=(whole, whole),
        scratch_shapes=scratch,
        compiler_params=pltpu.CompilerParams(
            collective_id=0, has_side_effects=True, vmem_limit_bytes=56 * 1024 * 1024
        ),
    )(*operands)


def solution(mesh):
    field = P(None, "lat", "lon", None)
    return jax.shard_map(
        functools.partial(per_device, mesh.shape["lat"], mesh.shape["lon"]),
        mesh=mesh,
        in_specs=(field, P(None, "lat", "lon")) + (P(),) * 11 + (field,),
        out_specs=(field, field),
        check_vma=False,
    )
```

time: 151 us -> 54.1 us (0.36)
  the two profiles are of different devices: /device:TPU:0 before, /device:TPU:1 now
where the time goes in v1:
time: 54.1 us; the launch traced here: 53.9 us
  Pallas kernels  45.3 us (84%)
  local copies, waits for them, and re-layouts  7.99 us (15%)
  between operations  0.64 us (1%)
    pallas_call x1, Pallas kernels, per_device(): pl.pallas_call(functools.partial(kernel, n_lat, n_lon), out_shape=(jax.Sh...  45.3 us
    unnamed x3, local copies, waits for them, and re-layouts  4.51 us
    pallas_call x2, local copies, waits for them, and re-layouts, per_device(): pl.pallas_call(functools.partial(kernel, n_lat, n_lon), out_shape=(jax.Sh...  3.48 us

profile of v1, /device:TPU:1, one launch (start us, length us, event | category | flops | bytes accessed | tf_op | source)
XLA Modules:
  0.0 53.9 jit_solution(6260386647501896830)
XLA Ops:
  0.6 1.3 %copy.19.labels = s32[2,6,12]{2,1,0:T(8,128)} copy(s32[2,6,12]{2,0,1:T(2,128)} %param.17) | data formatting | bytes 1152 | tf_op args[1]
  1.9 1.6 %copy.18.tokens = bf16[2,6,12,512]{3,2,1,0:T(8,128)(2,1)} copy(bf16[2,6,12,512]{3,0,2,1:T(2,128)(2,1)} %param.16) | data formatting | bytes 294912 | tf_op args[0]
  3.5 1.6 %copy.20.cotangent = bf16[2,6,12,512]{3,2,1,0:T(8,128)(2,1)} copy(bf16[2,6,12,512]{3,0,2,1:T(2,128)(2,1)} %param.29) | data formatting | bytes 294912 | tf_op args[13]
  5.1 45.3 %shard_map.167 = (bf16[2,6,12,512]{3,2,1,0:T(8,128)(2,1)}, bf16[2,6,12,512]{3,2,1,0:T(8,128)(2,1)}) custom-call(bf16[2,6,12,512]{3,2,1,0:T(8,128)(2,1)} %copy.18.tokens, s32[2,6,12]{2,1,0:T(8,128)} %copy.19.labels, f32[1,512]{1,0:T(1,128)} %bitcast.3, bf16[512,1536]{1,0:T(8,128)(2,1)} %project_one.1, bf16[512,512]{1,0:T(8,128)(2,1)} %output_one.1, ...), custom_call_target="tpu_custom_call" | custom-call | tf_op jit(solution)/shard_map/pallas_call | solution.py:350
  50.4 1.7 %copy.21 = bf16[2,6,12,512]{3,0,2,1:T(2,128)(2,1)} copy(bf16[2,6,12,512]{3,2,1,0:T(8,128)(2,1)} %get-tuple-element.2) | data formatting | bytes 294912 | tf_op jit(solution)/shard_map/pallas_call | solution.py:350
  52.2 1.7 %copy.22 = bf16[2,6,12,512]{3,0,2,1:T(2,128)(2,1)} copy(bf16[2,6,12,512]{3,2,1,0:T(8,128)(2,1)} %get-tuple-element.3) | data formatting | bytes 294912 | tf_op jit(solution)/shard_map/pallas_call | solution.py:350

commit v2 on v1

--- a/solution.py
+++ b/solution.py
@@ -15,7 +15,8 @@
 WLAT = 6
 WLON = 12
 LEV = 2
-WT = LEV * WLAT * WLON
+PLANE = WLAT * WLON
+WT = LEV * PLANE
 QUAD = WT // 4
 SLOT = 48
 ROWS = 4 * SLOT
@@ -132,7 +133,7 @@
     outputs, input_grad,
     tok, lab, g1, w1, wo1, b1, g2, w2, wo2, b2, g3, wup, wdn, cot, tq, fq,
     x, ct, packed_one, packed_two, probs_one, probs_two, heads_one, heads_two, d_heads, d_packed,
-    middle, hat_one, hat_two, u_keep, dh_keep, result, allowed_ref,
+    hat_one, hat_two, hidden, dh_keep, allowed_ref,
     out_stage, grad_stage,
     send, recv, lab_send, lab_recv,
     load_sem, send_sem, recv_sem, lab_send_sem, lab_recv_sem, out_sem,
@@ -161,14 +162,21 @@
     masks = head_masks()
 
     def to_rows(source, target):
-        for a in range(LEV):
-            for b in range(WLAT):
-                target[pl.ds((a * WLAT + b) * WLON, WLON), :] = source[a, b].astype(F32)
-
-    owner_target = {0: (north, west), 1: (north, j), 2: (i, west)}
-    window_target = {3: (south, east), 2: (south, j), 1: (i, east)}
-
-    def exchange(step, targets):
+        for level in range(LEV):
+            target[pl.ds(PLANE * level, PLANE), :] = source[:, level, :].astype(F32)
+
+    def to_cells(value, target):
+        for level in range(LEV):
+            target[:, level, :] = value[PLANE * level : PLANE * (level + 1)].astype(BF)
+
+    owner_target = {0: (north, west), 2: (i, west), 1: (north, j)}
+    window_target = {3: (south, east), 1: (i, east), 2: (south, j)}
+
+    def start(step, targets, value):
+        rows = nn(tq[...], value).astype(BF)
+        send[step] = rows
+        stay = 3 if targets is owner_target else 0
+        recv[step, pl.ds(SLOT * (3 - stay), SLOT)] = rows[SLOT * stay : SLOT * (stay + 1)]
         copies = []
         for q, device in targets.items():
             copies.append(
@@ -181,22 +189,13 @@
                     device_id_type=MESH,
                 )
             )
-        return copies
-
-    def start(step, targets, value):
-        rows = nn(tq[...], value).astype(BF)
-        send[step] = rows
-        stay = 3 if step % 2 == 0 else 0
-        recv[step, pl.ds(SLOT * (3 - stay), SLOT)] = rows[SLOT * stay : SLOT * (stay + 1)]
-        copies = exchange(step, targets)
-        for copy in copies:
-            copy.start()
+            copies[-1].start()
         return copies
 
     def arrived(step, copies):
         for copy in copies:
             copy.wait_recv()
-        return nn(fq[...], recv[step]).astype(BF)
+        return nn(fq[...], recv[step])
 
     loads["tok"].wait()
     to_rows(tok, x)
@@ -207,21 +206,21 @@
     loads["w1"].wait()
     packed_one[...] = nn(normed, w1[...]).astype(BF)
 
-    loads["lab"].wait()
-    loads["tq"].wait()
-    loads["fq"].wait()
+    for name in ("lab", "tq", "fq", "cot"):
+        loads[name].wait()
     token = lax.broadcasted_iota(jnp.int32, (WT, WLON), 0)
     column = lax.broadcasted_iota(jnp.int32, (WT, WLON), 1)
     labelled = jnp.zeros((WT, WLON), F32)
-    for a in range(LEV):
-        level = lab[a].astype(F32)
-        for b in range(WLAT):
-            line = jnp.broadcast_to(level[b : b + 1, :], (WT, WLON))
+    for b in range(WLAT):
+        line_pair = lab[b].astype(F32)
+        for a in range(LEV):
+            line = jnp.broadcast_to(line_pair[a : a + 1, :], (WT, WLON))
             labelled = jnp.where(token - (a * WLAT + b) * WLON == column, line, labelled)
     label_col = jnp.sum(labelled, axis=-1, keepdims=True)
     label_rows = nn(tq[...], jnp.broadcast_to(label_col, (WT, LANES)).astype(BF)).astype(BF)
     lab_send[...] = label_rows
     lab_recv[pl.ds(0, SLOT)] = label_rows[3 * SLOT :]
+    to_rows(cot, ct)
     pl.semaphore_wait(barrier, len(around))
     lab_copies = []
     for q, device in owner_target.items():
@@ -236,46 +235,37 @@
             )
         )
         lab_copies[-1].start()
+    cot_copies = start(0, owner_target, ct[...].astype(BF))
 
     loads["b1"].wait()
     attention(packed_one, b1, probs_one, heads_one, None, masks)
     loads["wo1"].wait()
-    mid = x[...] + nn(heads_one[...], wo1[...])
-    middle[...] = mid
-    hat, rs_two = norm_parts(mid)
-    hat_two[...] = hat
-    loads["g2"].wait()
-    copies_0 = start(0, owner_target, (hat * g2[...]).astype(BF))
-
-    loads["cot"].wait()
-    to_rows(cot, ct)
+    mid_copies = start(1, owner_target, (x[...] + nn(heads_one[...], wo1[...])).astype(BF))
+
+    ct[...] = arrived(0, cot_copies)
     loads["wdn"].wait()
     dh_keep[...] = nt(ct[...].astype(BF), wdn[...]).astype(BF)
     for copy in lab_copies:
         copy.wait_recv()
     label_here = nn(fq[...], lab_recv[...])
     row = lax.broadcasted_iota(jnp.int32, (WT, LANES), 0)
-    half = WLAT * WLON
     late_row = jnp.logical_or(
-        jnp.logical_and(row >= half // 2, row < half), row >= half + half // 2
+        jnp.logical_and(row >= PLANE // 2, row < PLANE), row >= PLANE + PLANE // 2
     )
     edge = jnp.where(i == n_lat - 1, 1.0, 0.0).astype(F32)
     ids = label_here * 2.0 + jnp.where(late_row, edge, 0.0)
     lane = lax.broadcasted_iota(jnp.int32, (WT, LANES), 1).astype(F32)
     one_hot = jnp.where(ids == lane, 1.0, 0.0).astype(BF)
     allowed_ref[...] = nt(one_hot, one_hot)
-
-    loads["w2"].wait()
-    loads["b2"].wait()
-    normed = arrived(0, copies_0)
-
-    packed_two[...] = nn(normed, w2[...]).astype(BF)
+    for name in ("g2", "w2", "b2", "wo2", "g3", "wup"):
+        loads[name].wait()
+
+    mid = arrived(1, mid_copies)
+    hat, rs_two = norm_parts(mid)
+    hat_two[...] = hat
+    packed_two[...] = nn((hat * g2[...]).astype(BF), w2[...]).astype(BF)
     attention(packed_two, b2, probs_two, heads_two, allowed_ref[...], masks)
-    copies_1 = start(1, window_target, heads_two[...])
-    loads["wo2"].wait()
-    loads["g3"].wait()
-    loads["wup"].wait()
-    late = middle[...] + nn(arrived(1, copies_1), wo2[...])
+    late = mid + nn(heads_two[...], wo2[...])
 
     hat, rs_three = norm_parts(late)
     u = nn((hat * g3[...]).astype(BF), wup[...])
@@ -286,35 +276,28 @@
         1.0 + (3.0 * 0.044715) * square
     )
     du = (dh_keep[...].astype(F32) * slope).astype(BF)
-    hidden = (0.5 * u * (1.0 + bent)).astype(BF)
-    u_keep[...] = hidden
+    hidden[...] = (0.5 * u * (1.0 + bent)).astype(BF)
     dn = nt(du, wup[...]).astype(BF).astype(F32)
     d_late = ct[...] + norm_back(hat, rs_three, g3[...], dn)
-    copies_2 = start(2, owner_target, nt(d_late.astype(BF), wo2[...]).astype(BF))
-
-    result[...] = late + nn(u_keep[...], wdn[...])
-    for a in range(LEV):
-        for b in range(WLAT):
-            out_stage[a, b] = result[pl.ds((a * WLAT + b) * WLON, WLON), :].astype(BF)
+
+    d_heads[...] = nt(d_late.astype(BF), wo2[...]).astype(BF)
+    attention_back(packed_two, probs_two, heads_two, d_heads, d_packed, masks)
+    dn = nt(d_packed[...], w2[...]).astype(BF).astype(F32)
+    d_mid = d_late + norm_back(hat_two[...], rs_two, g2[...], dn)
+    back_copies = start(2, window_target, d_mid.astype(BF))
+    out_copies = start(3, window_target, (late + nn(hidden[...], wdn[...])).astype(BF))
+
+    d_mid = arrived(2, back_copies)
+    d_heads[...] = nt(d_mid.astype(BF), wo1[...]).astype(BF)
+    attention_back(packed_one, probs_one, heads_one, d_heads, d_packed, masks)
+    to_cells(arrived(3, out_copies), out_stage)
     out_copy = pltpu.make_async_copy(out_stage, outputs, out_sem.at[0])
     out_copy.start()
-
-    d_heads[...] = arrived(2, copies_2)
-    attention_back(packed_two, probs_two, heads_two, d_heads, d_packed, masks)
-    copies_3 = start(3, window_target, nt(d_packed[...], w2[...]).astype(BF))
-    dn = arrived(3, copies_3).astype(F32)
-    d_mid = d_late + norm_back(hat_two[...], rs_two, g2[...], dn)
-
-    d_heads[...] = nt(d_mid.astype(BF), wo1[...]).astype(BF)
-    attention_back(packed_one, probs_one, heads_one, d_heads, d_packed, masks)
     dn = nt(d_packed[...], w1[...]).astype(BF).astype(F32)
-    result[...] = d_mid + norm_back(hat_one[...], rs_one, g1[...], dn)
-    for a in range(LEV):
-        for b in range(WLAT):
-            grad_stage[a, b] = result[pl.ds((a * WLAT + b) * WLON, WLON), :].astype(BF)
+    to_cells(d_mid + norm_back(hat_one[...], rs_one, g1[...], dn), grad_stage)
     grad_copy = pltpu.make_async_copy(grad_stage, input_grad, out_sem.at[1])
     grad_copy.start()
-    for copy in lab_copies + copies_0 + copies_1 + copies_2 + copies_3:
+    for copy in lab_copies + cot_copies + mid_copies + back_copies + out_copies:
         copy.wait_send()
     out_copy.wait()
     grad_copy.wait()
@@ -325,20 +308,22 @@
     place = quadrant_matrix()
     to_quad = jnp.asarray(place, BF)
     from_quad = jnp.asarray(place.T, BF)
+    def cells(a):
+        return a.transpose(1, 2, 0, 3).reshape(PLANE, LEV, D)
+
     operands = (
-        tokens, labels, g1.reshape(1, D), w1, wo1, b1, g2.reshape(1, D), w2, wo2, b2,
-        g3.reshape(1, D), wup, wdn, cot, to_quad, from_quad,
+        cells(tokens), labels.transpose(1, 0, 2), g1.reshape(1, D), w1, wo1, b1, g2.reshape(1, D), w2, wo2, b2,
+        g3.reshape(1, D), wup, wdn, cells(cot), to_quad, from_quad,
     )
     vm = pltpu.VMEM
     landing = [vm(a.shape, a.dtype) for a in operands]
-    block = tokens.shape
+    block = (PLANE, LEV, D)
     scratch = landing + [
         vm((WT, D), F32), vm((WT, D), F32),
         vm((WT, 3 * D), BF), vm((WT, 3 * D), BF),
         vm((HEADS * WT, WT), BF), vm((HEADS * WT, WT), BF),
         vm((WT, D), BF), vm((WT, D), BF), vm((WT, D), BF), vm((WT, 3 * D), BF),
-        vm((WT, D), F32), vm((WT, D), F32), vm((WT, D), F32),
-        vm((WT, FF), BF), vm((WT, FF), BF), vm((WT, D), F32), vm((WT, WT), F32),
+        vm((WT, D), F32), vm((WT, D), F32), vm((WT, FF), BF), vm((WT, FF), BF), vm((WT, WT), F32),
         vm(block, BF), vm(block, BF),
         vm((4, ROWS, D), BF), vm((4, ROWS, D), BF), vm((ROWS, LANES), BF), vm((ROWS, LANES), BF),
         pltpu.SemaphoreType.DMA((len(operands),)),
@@ -347,7 +332,7 @@
         pltpu.SemaphoreType.DMA((2,)),
     ]
     whole = pl.BlockSpec(memory_space=pl.ANY)
-    return pl.pallas_call(
+    results = pl.pallas_call(
         functools.partial(kernel, n_lat, n_lon),
         out_shape=(jax.ShapeDtypeStruct(block, BF), jax.ShapeDtypeStruct(block, BF)),
         in_specs=[whole] * len(operands),
@@ -357,6 +342,7 @@
             collective_id=0, has_side_effects=True, vmem_limit_bytes=56 * 1024 * 1024
         ),
     )(*operands)
+    return tuple(a.reshape(WLAT, WLON, LEV, D).transpose(2, 0, 1, 3) for a in results)
 
 
 def solution(mesh):

time: 54.1 us -> 39.1 us (0.72)
  Pallas kernels: 45.3 us -> 34.9 us
  local copies, waits for them, and re-layouts: 7.99 us -> 3.35 us
    pallas_call x1, Pallas kernels: 45.3 us -> 34.9 us  [per_device(): pl.pallas_call(functools.partial(kernel, n_lat, n_lon), out_shape=(jax.Sh...]
    pallas_call x2 -> x0, local copies, waits for them, and re-layouts: 3.48 us -> none  [per_device(): pl.pallas_call(functools.partial(kernel, n_lat, n_lon), out_shape=(jax.Sh...]
    unnamed x3 -> x2, local copies, waits for them, and re-layouts: 4.51 us -> 3.35 us
where the time goes in v2:
time: 39.1 us; the launch traced here: 38.9 us
  Pallas kernels  34.9 us (89%)
  local copies, waits for them, and re-layouts  3.35 us (9%)
  between operations  0.64 us (2%)
    pallas_call x1, Pallas kernels, per_device(): pl.pallas_call(functools.partial(kernel, n_lat, n_lon), out_shape=(jax.Sh...  34.9 us
    unnamed x2, local copies, waits for them, and re-layouts  3.35 us

profile of v2, /device:TPU:1, one launch (start us, length us, event | category | flops | bytes accessed | tf_op | source)
XLA Modules:
  0.0 38.9 jit_solution(16888947598745253148)
XLA Ops:
  0.6 34.9 %shard_map.167 = (bf16[72,2,512]{2,1,0:T(2,128)(2,1)}, bf16[72,2,512]{2,1,0:T(2,128)(2,1)}) custom-call(bf16[72,2,512]{2,1,0:T(2,128)(2,1)} %bitcast.18, s32[6,2,12]{2,1,0:T(2,128)} %bitcast.20, f32[1,512]{1,0:T(1,128)} %bitcast.21, bf16[512,1536]{1,0:T(8,128)(2,1)} %project_one.1, bf16[512,512]{1,0:T(8,128)(2,1)} %output_one.1, ...), custom_call_target="tpu_custom_call" | custom-call | tf_op jit(solution)/shard_map/pallas_call | solution.py:335
  35.5 1.7 %copy.20 = bf16[2,6,12,512]{3,0,2,1:T(2,128)(2,1)} copy(bf16[2,6,12,512]{3,0,2,1:T(2,128)(2,1)} %bitcast.17) | data formatting | bytes 294912
  37.2 1.7 %copy.21 = bf16[2,6,12,512]{3,0,2,1:T(2,128)(2,1)} copy(bf16[2,6,12,512]{3,0,2,1:T(2,128)(2,1)} %bitcast.16) | data formatting | bytes 294912

commit v3 on v2

--- a/solution.py
+++ b/solution.py
@@ -169,13 +169,13 @@
         for level in range(LEV):
             target[:, level, :] = value[PLANE * level : PLANE * (level + 1)].astype(BF)
 
-    owner_target = {0: (north, west), 2: (i, west), 1: (north, j)}
-    window_target = {3: (south, east), 1: (i, east), 2: (south, j)}
+    owner_target = {3: (south, east), 1: (i, east), 2: (south, j)}
+    window_target = {0: (north, west), 2: (i, west), 1: (north, j)}
 
     def start(step, targets, value):
         rows = nn(tq[...], value).astype(BF)
         send[step] = rows
-        stay = 3 if targets is owner_target else 0
+        stay = 0 if targets is owner_target else 3
         recv[step, pl.ds(SLOT * (3 - stay), SLOT)] = rows[SLOT * stay : SLOT * (stay + 1)]
         copies = []
         for q, device in targets.items():
@@ -219,7 +219,7 @@
     label_col = jnp.sum(labelled, axis=-1, keepdims=True)
     label_rows = nn(tq[...], jnp.broadcast_to(label_col, (WT, LANES)).astype(BF)).astype(BF)
     lab_send[...] = label_rows
-    lab_recv[pl.ds(0, SLOT)] = label_rows[3 * SLOT :]
+    lab_recv[pl.ds(3 * SLOT, SLOT)] = label_rows[:SLOT]
     to_rows(cot, ct)
     pl.semaphore_wait(barrier, len(around))
     lab_copies = []
@@ -252,7 +252,7 @@
     late_row = jnp.logical_or(
         jnp.logical_and(row >= PLANE // 2, row < PLANE), row >= PLANE + PLANE // 2
     )
-    edge = jnp.where(i == n_lat - 1, 1.0, 0.0).astype(F32)
+    edge = jnp.where(i == 0, 1.0, 0.0).astype(F32)
     ids = label_here * 2.0 + jnp.where(late_row, edge, 0.0)
     lane = lax.broadcasted_iota(jnp.int32, (WT, LANES), 1).astype(F32)
     one_hot = jnp.where(ids == lane, 1.0, 0.0).astype(BF)
@@ -301,6 +301,11 @@
         copy.wait_send()
     out_copy.wait()
     grad_copy.wait()
+
+
+def write_out(first, second, first_out, second_out):
+    first_out[...] = first[...]
+    second_out[...] = second[...]
 
 
 def per_device(n_lat, n_lon, *args):
@@ -342,6 +347,12 @@
             collective_id=0, has_side_effects=True, vmem_limit_bytes=56 * 1024 * 1024
         ),
     )(*operands)
+    results = pl.pallas_call(
+        write_out,
+        out_shape=(jax.ShapeDtypeStruct(block, BF), jax.ShapeDtypeStruct(block, BF)),
+        in_specs=[pl.BlockSpec(memory_space=pltpu.VMEM)] * 2,
+        out_specs=[pl.BlockSpec(memory_space=pltpu.VMEM)] * 2,
+    )(*results)
     return tuple(a.reshape(WLAT, WLON, LEV, D).transpose(2, 0, 1, 3) for a in results)
 
 

time: 39.1 us -> 36.3 us (0.928)
  local copies, waits for them, and re-layouts: 3.35 us -> 0 us
  Pallas kernels: 34.9 us -> 35.5 us
    unnamed x2 -> x0, local copies, waits for them, and re-layouts: 3.35 us -> none
    pallas_call x0 -> x1, Pallas kernels: none -> 1.7 us  [per_device(): pl.pallas_call(write_out, out_shape=(jax.ShapeDtypeStruct(block, BF), jax...]
    pallas_call x1, Pallas kernels: 34.9 us -> 33.8 us  [per_device(): pl.pallas_call(functools.partial(kernel, n_lat, n_lon), out_shape=(jax.Sh...]
where the time goes in v3:
time: 36.3 us; the launch traced here: 36.2 us
  Pallas kernels  35.5 us (98%)
  between operations  0.64 us (2%)
    pallas_call x1, Pallas kernels, per_device(): pl.pallas_call(functools.partial(kernel, n_lat, n_lon), out_shape=(jax.Sh...  33.8 us
    pallas_call x1, Pallas kernels, per_device(): pl.pallas_call(write_out, out_shape=(jax.ShapeDtypeStruct(block, BF), jax...  1.7 us

profile of v3, /device:TPU:1, one launch (start us, length us, event | category | flops | bytes accessed | tf_op | source)
XLA Modules:
  0.0 36.2 jit_solution(3266415181485612278)
XLA Ops:
  0.6 33.8 %shard_map.167 = (bf16[72,2,512]{2,1,0:T(2,128)(2,1)}, bf16[72,2,512]{2,1,0:T(2,128)(2,1)}) custom-call(bf16[72,2,512]{2,1,0:T(2,128)(2,1)} %bitcast.16, s32[6,2,12]{2,1,0:T(2,128)} %bitcast.18, f32[1,512]{1,0:T(1,128)} %bitcast.19, bf16[512,1536]{1,0:T(8,128)(2,1)} %project_one.1, bf16[512,512]{1,0:T(8,128)(2,1)} %output_one.1, ...), custom_call_target="tpu_custom_call" | custom-call | tf_op jit(solution)/shard_map/pallas_call | solution.py:340
  34.5 1.7 %shard_map.168 = (bf16[72,2,512]{2,1,0:T(2,128)(2,1)}, bf16[72,2,512]{2,1,0:T(2,128)(2,1)}) custom-call(bf16[72,2,512]{2,1,0:T(2,128)(2,1)} %get-tuple-element.6.first, bf16[72,2,512]{2,1,0:T(2,128)(2,1)} %get-tuple-element.7.second), custom_call_target="tpu_custom_call" | custom-call | tf_op jit(solution)/shard_map/pallas_call | solution.py:350

commit v4 on v3

--- a/solution.py
+++ b/solution.py
@@ -22,6 +22,7 @@
 ROWS = 4 * SLOT
 D = 512
 FF = 2048
+CHUNK = 256
 HEADS = 16
 HD = D // HEADS
 LANES = 128
@@ -29,6 +30,8 @@
 GROUPS = D // LANES
 SCALE = HD ** (-0.5)
 EPSILON = 1e-05
+LOG2E = 1.4426950408889634
+TILE = 16
 
 
 def quadrant_matrix():
@@ -39,7 +42,9 @@
             for i in range(QUAD):
                 level, r, c = i // (hl * hc), i // hc % hl, i % hc
                 token = level * WLAT * WLON + (half_row * hl + r) * WLON + half_col * hc + c
-                place[SLOT * (2 * half_row + half_col) + i, token] = 1.0
+                first = SLOT * (2 * half_row + half_col) + i
+                for row in [first] if i < 32 else range(first, first + 16, 4):
+                    place[row, token] = 1.0
     return place
 
 
@@ -85,45 +90,78 @@
     return jnp.concatenate([jnp.where(m, group, zero) for m in masks], axis=0)
 
 
-def attention(packed, bias, probs, heads, allowed, masks):
+def group(packed, g):
+    return [packed[:, D * n + LANES * g : D * n + LANES * (g + 1)] for n in range(3)]
+
+
+def attention(packed, weight_of, probs, heads, inverse, masks):
+    def score(g):
+        q, k, _ = group(packed, g)
+        return nt(spread(q, masks), k)
+
+    ahead = score(0)
     for g in range(GROUPS):
-        lanes = slice(LANES * g, LANES * (g + 1))
-        q = packed[:, LANES * g : LANES * (g + 1)]
-        k = packed[:, D + LANES * g : D + LANES * (g + 1)]
-        v = packed[:, 2 * D + LANES * g : 2 * D + LANES * (g + 1)]
-        s = nt(spread(q, masks), k)
+        s = ahead
+        if g + 1 < GROUPS:
+            ahead = score(g + 1)
+        v = group(packed, g)[2]
+        parts = []
         for j in range(PER):
             h = PER * g + j
-            e = jnp.exp(s[WT * j : WT * (j + 1)] * SCALE + bias[h].astype(F32))
-            if allowed is not None:
-                e = e * allowed
-            z = jnp.sum(e, axis=-1, keepdims=True)
-            down = jnp.where(z > 2.0**64, 2.0**-64, 1.0).astype(F32)
-            probs[pl.ds(WT * h, WT), :] = ((e * down) * (1.0 / (z * down))).astype(BF)
-        o = nn(probs[pl.ds(WT * PER * g, WT * PER), :], v)
-        heads[:, lanes] = pick(o, masks).astype(BF)
-
-
-def attention_back(packed, probs, heads, d_heads, d_packed, masks):
+            parts.append(weight_of(s[WT * j : WT * (j + 1)], h).astype(BF))
+            probs[pl.ds(WT * h, WT), :] = parts[-1]
+        o = nn(jnp.concatenate(parts, axis=0), jnp.concatenate([v, jnp.ones_like(v)], axis=1))
+        inv = 1.0 / pick(o[:, LANES:], masks)
+        heads[:, LANES * g : LANES * (g + 1)] = (pick(o[:, :LANES], masks) * inv).astype(BF)
+        inverse[:, LANES * g : LANES * (g + 1)] = inv
+
+
+def attention_back(packed, probs, heads, inverse, d_heads, d_packed, masks):
+    def first(g):
+        lanes = slice(LANES * g, LANES * (g + 1))
+        v = group(packed, g)[2]
+        do = d_heads[:, lanes].astype(F32) * inverse[:, lanes]
+        less = (-(do * heads[:, lanes].astype(F32))).astype(BF)
+        do = spread(do.astype(BF), masks)
+        left = jnp.concatenate([do, spread(less, masks)], axis=1)
+        return do, nt(left, jnp.concatenate([v, jnp.ones_like(v)], axis=1))
+
+    ahead = [first(0), first(1)]
     for g in range(GROUPS):
-        q = packed[:, LANES * g : LANES * (g + 1)]
-        k = packed[:, D + LANES * g : D + LANES * (g + 1)]
-        v = packed[:, 2 * D + LANES * g : 2 * D + LANES * (g + 1)]
-        do = d_heads[:, LANES * g : LANES * (g + 1)]
-        o = heads[:, LANES * g : LANES * (g + 1)]
-        less = (-(do.astype(F32) * o.astype(F32))).astype(BF)
-        do_stack = spread(do, masks)
-        left = jnp.concatenate([do_stack, spread(less, masks)], axis=1)
-        right = jnp.concatenate([v, jnp.ones_like(v)], axis=1)
-        dp = nt(left, right)
+        do, dp = ahead.pop(0)
+        if g + 2 < GROUPS:
+            ahead.append(first(g + 2))
+        q, k, _ = group(packed, g)
         p = probs[pl.ds(WT * PER * g, WT * PER), :]
+        dv = tn(p, do)
         ds = (p.astype(F32) * dp).astype(BF)
+        dk = tn(ds, spread(q, masks)) * SCALE
         dq = pick(nn(ds, k), masks) * SCALE
-        dk = tn(ds, spread(q, masks)) * SCALE
-        dv = tn(p, do_stack)
-        d_packed[:, LANES * g : LANES * (g + 1)] = dq.astype(BF)
-        d_packed[:, D + LANES * g : D + LANES * (g + 1)] = dk.astype(BF)
-        d_packed[:, 2 * D + LANES * g : 2 * D + LANES * (g + 1)] = dv.astype(BF)
+        for n, part in enumerate((dq, dk, dv)):
+            d_packed[:, D * n + LANES * g : D * n + LANES * (g + 1)] = part.astype(BF)
+
+
+def feed_gradient(normed, up, up_t, half_dh, hidden):
+    root = (2.0 / np.pi) ** 0.5
+
+    def lift(c):
+        return nn(normed, up[:, CHUNK * c : CHUNK * (c + 1)])
+
+    total = None
+    ahead = lift(0)
+    for c in range(FF // CHUNK):
+        u = ahead
+        if c + 1 < FF // CHUNK:
+            ahead = lift(c + 1)
+        lanes = slice(CHUNK * c, CHUNK * (c + 1))
+        cubic = (u * u) * (root * 0.044715)
+        bent = jnp.tanh(u * (cubic + root))
+        above = 1.0 + bent
+        slope = above * (1.0 + (u * (3.0 * cubic + root)) * (1.0 - bent))
+        hidden[:, lanes] = (0.5 * u * above).astype(BF)
+        part = nn((half_dh[:, lanes].astype(F32) * slope).astype(BF), up_t[lanes, :])
+        total = part if total is None else total + part
+    return total
 
 
 def kernel(
@@ -133,7 +171,7 @@
     outputs, input_grad,
     tok, lab, g1, w1, wo1, b1, g2, w2, wo2, b2, g3, wup, wdn, cot, tq, fq,
     x, ct, packed_one, packed_two, probs_one, probs_two, heads_one, heads_two, d_heads, d_packed,
-    hat_one, hat_two, hidden, dh_keep, allowed_ref,
+    hat_one, hat_two, inv_one, inv_two, hidden, dh_keep, table_two, w1t, wo1t, w2t, wo2t, wupt,
     out_stage, grad_stage,
     send, recv, lab_send, lab_recv,
     load_sem, send_sem, recv_sem, lab_send_sem, lab_recv_sem, out_sem,
@@ -172,17 +210,39 @@
     owner_target = {3: (south, east), 1: (i, east), 2: (south, j)}
     window_target = {0: (north, west), 2: (i, west), 1: (north, j)}
 
+    quarter = lax.broadcasted_iota(jnp.int32, (TILE, LANES), 0)
+    quarters = [
+        jnp.logical_and(quarter >= 4 * k, quarter < 4 * (k + 1)) for k in range(GROUPS)
+    ]
+
+    def pack(target, rows):
+        for a in range(2):
+            for k in range(GROUPS):
+                target[4 * a + k] = rows[TILE * a : TILE * (a + 1), LANES * k : LANES * (k + 1)]
+        rest = rows[2 * TILE : SLOT]
+        last = rest[:, :LANES]
+        for k in range(1, GROUPS):
+            last = jnp.where(quarters[k], rest[:, LANES * k : LANES * (k + 1)], last)
+        target[8] = last
+
+    def unpack(source):
+        rows = [
+            jnp.concatenate([source[4 * a + k] for k in range(GROUPS)], axis=1) for a in range(2)
+        ]
+        last = source[8]
+        zero = jnp.zeros_like(last)
+        rows.append(jnp.concatenate([jnp.where(m, last, zero) for m in quarters], axis=1))
+        return jnp.concatenate(rows, axis=0)
+
     def start(step, targets, value):
         rows = nn(tq[...], value).astype(BF)
-        send[step] = rows
-        stay = 0 if targets is owner_target else 3
-        recv[step, pl.ds(SLOT * (3 - stay), SLOT)] = rows[SLOT * stay : SLOT * (stay + 1)]
         copies = []
         for q, device in targets.items():
+            pack(send.at[step, q], rows[SLOT * q : SLOT * (q + 1)])
             copies.append(
                 pltpu.make_async_remote_copy(
-                    src_ref=send.at[step, pl.ds(SLOT * q, SLOT)],
-                    dst_ref=recv.at[step, pl.ds(SLOT * (3 - q), SLOT)],
+                    src_ref=send.at[step, q],
+                    dst_ref=recv.at[step, 3 - q],
                     send_sem=send_sem.at[step, q],
                     recv_sem=recv_sem.at[step, q],
                     device_id=device,
@@ -190,12 +250,14 @@
                 )
             )
             copies[-1].start()
+        stay = 0 if targets is owner_target else 3
+        pack(recv.at[step, 3 - stay], rows[SLOT * stay : SLOT * (stay + 1)])
         return copies
 
     def arrived(step, copies):
         for copy in copies:
             copy.wait_recv()
-        return nn(fq[...], recv[step])
+        return nn(fq[...], jnp.concatenate([unpack(recv.at[step, q]) for q in range(4)], axis=0))
 
     loads["tok"].wait()
     to_rows(tok, x)
@@ -217,7 +279,12 @@
             line = jnp.broadcast_to(line_pair[a : a + 1, :], (WT, WLON))
             labelled = jnp.where(token - (a * WLAT + b) * WLON == column, line, labelled)
     label_col = jnp.sum(labelled, axis=-1, keepdims=True)
-    label_rows = nn(tq[...], jnp.broadcast_to(label_col, (WT, LANES)).astype(BF)).astype(BF)
+    label_rows = nn(tq[...], jnp.broadcast_to(label_col, (WT, LANES)).astype(BF))
+    row = lax.broadcasted_iota(jnp.int32, (ROWS, LANES), 0)
+    for q in range(4):
+        spare = jnp.logical_and(row >= SLOT * q + QUAD, row < SLOT * (q + 1))
+        label_rows = jnp.where(spare, 0.0, label_rows)
+    label_rows = label_rows.astype(BF)
     lab_send[...] = label_rows
     lab_recv[pl.ds(3 * SLOT, SLOT)] = label_rows[:SLOT]
     to_rows(cot, ct)
@@ -238,13 +305,22 @@
     cot_copies = start(0, owner_target, ct[...].astype(BF))
 
     loads["b1"].wait()
-    attention(packed_one, b1, probs_one, heads_one, None, masks)
+
+    def weight_one(score, h):
+        t = score * SCALE + b1[h].astype(F32)
+        return jnp.exp(t - jnp.max(t, axis=-1, keepdims=True))
+
+    def weight_two(score, h):
+        t = score * (SCALE * LOG2E) + table_two[h]
+        return jnp.exp2(t - jnp.max(t, axis=-1, keepdims=True))
+
+    attention(packed_one, weight_one, probs_one, heads_one, inv_one, masks)
     loads["wo1"].wait()
     mid_copies = start(1, owner_target, (x[...] + nn(heads_one[...], wo1[...])).astype(BF))
 
     ct[...] = arrived(0, cot_copies)
     loads["wdn"].wait()
-    dh_keep[...] = nt(ct[...].astype(BF), wdn[...]).astype(BF)
+    dh_keep[...] = (0.5 * nt(ct[...].astype(BF), wdn[...])).astype(BF)
     for copy in lab_copies:
         copy.wait_recv()
     label_here = nn(fq[...], lab_recv[...])
@@ -256,44 +332,41 @@
     ids = label_here * 2.0 + jnp.where(late_row, edge, 0.0)
     lane = lax.broadcasted_iota(jnp.int32, (WT, LANES), 1).astype(F32)
     one_hot = jnp.where(ids == lane, 1.0, 0.0).astype(BF)
-    allowed_ref[...] = nt(one_hot, one_hot)
-    for name in ("g2", "w2", "b2", "wo2", "g3", "wup"):
+    barred = (nt(one_hot, one_hot) - 1.0) * 1e30
+    loads["b2"].wait()
+    for h in range(HEADS):
+        table_two[h] = b2[h].astype(F32) * LOG2E + barred
+    for name in ("g2", "w2", "wo2", "g3", "wup"):
         loads[name].wait()
+    for weight, turned in ((wup, wupt), (w2, w2t), (wo2, wo2t), (w1, w1t), (wo1, wo1t)):
+        turned[...] = weight[...].T
 
     mid = arrived(1, mid_copies)
     hat, rs_two = norm_parts(mid)
     hat_two[...] = hat
     packed_two[...] = nn((hat * g2[...]).astype(BF), w2[...]).astype(BF)
-    attention(packed_two, b2, probs_two, heads_two, allowed_ref[...], masks)
+    attention(packed_two, weight_two, probs_two, heads_two, inv_two, masks)
     late = mid + nn(heads_two[...], wo2[...])
 
     hat, rs_three = norm_parts(late)
-    u = nn((hat * g3[...]).astype(BF), wup[...])
-    root = (2.0 / np.pi) ** 0.5
-    square = u * u
-    bent = jnp.tanh(root * u * (1.0 + 0.044715 * square))
-    slope = 0.5 * (1.0 + bent) + (0.5 * root) * u * (1.0 - bent * bent) * (
-        1.0 + (3.0 * 0.044715) * square
-    )
-    du = (dh_keep[...].astype(F32) * slope).astype(BF)
-    hidden[...] = (0.5 * u * (1.0 + bent)).astype(BF)
-    dn = nt(du, wup[...]).astype(BF).astype(F32)
+    normed = (hat * g3[...]).astype(BF)
+    dn = feed_gradient(normed, wup, wupt, dh_keep, hidden).astype(BF).astype(F32)
     d_late = ct[...] + norm_back(hat, rs_three, g3[...], dn)
 
-    d_heads[...] = nt(d_late.astype(BF), wo2[...]).astype(BF)
-    attention_back(packed_two, probs_two, heads_two, d_heads, d_packed, masks)
-    dn = nt(d_packed[...], w2[...]).astype(BF).astype(F32)
+    d_heads[...] = nn(d_late.astype(BF), wo2t[...]).astype(BF)
+    attention_back(packed_two, probs_two, heads_two, inv_two, d_heads, d_packed, masks)
+    dn = nn(d_packed[...], w2t[...]).astype(BF).astype(F32)
     d_mid = d_late + norm_back(hat_two[...], rs_two, g2[...], dn)
     back_copies = start(2, window_target, d_mid.astype(BF))
     out_copies = start(3, window_target, (late + nn(hidden[...], wdn[...])).astype(BF))
 
     d_mid = arrived(2, back_copies)
-    d_heads[...] = nt(d_mid.astype(BF), wo1[...]).astype(BF)
-    attention_back(packed_one, probs_one, heads_one, d_heads, d_packed, masks)
+    d_heads[...] = nn(d_mid.astype(BF), wo1t[...]).astype(BF)
+    attention_back(packed_one, probs_one, heads_one, inv_one, d_heads, d_packed, masks)
     to_cells(arrived(3, out_copies), out_stage)
     out_copy = pltpu.make_async_copy(out_stage, outputs, out_sem.at[0])
     out_copy.start()
-    dn = nt(d_packed[...], w1[...]).astype(BF).astype(F32)
+    dn = nn(d_packed[...], w1t[...]).astype(BF).astype(F32)
     to_cells(d_mid + norm_back(hat_one[...], rs_one, g1[...], dn), grad_stage)
     grad_copy = pltpu.make_async_copy(grad_stage, input_grad, out_sem.at[1])
     grad_copy.start()
@@ -328,9 +401,11 @@
         vm((WT, 3 * D), BF), vm((WT, 3 * D), BF),
         vm((HEADS * WT, WT), BF), vm((HEADS * WT, WT), BF),
         vm((WT, D), BF), vm((WT, D), BF), vm((WT, D), BF), vm((WT, 3 * D), BF),
-        vm((WT, D), F32), vm((WT, D), F32), vm((WT, FF), BF), vm((WT, FF), BF), vm((WT, WT), F32),
+        vm((WT, D), F32), vm((WT, D), F32), vm((WT, D), F32), vm((WT, D), F32),
+        vm((WT, FF), BF), vm((WT, FF), BF), vm((HEADS, WT, WT), F32),
+        vm((3 * D, D), BF), vm((D, D), BF), vm((3 * D, D), BF), vm((D, D), BF), vm((FF, D), BF),
         vm(block, BF), vm(block, BF),
-        vm((4, ROWS, D), BF), vm((4, ROWS, D), BF), vm((ROWS, LANES), BF), vm((ROWS, LANES), BF),
+        vm((4, 4, 9, TILE, LANES), BF), vm((4, 4, 9, TILE, LANES), BF), vm((ROWS, LANES), BF), vm((ROWS, LANES), BF),
         pltpu.SemaphoreType.DMA((len(operands),)),
         pltpu.SemaphoreType.DMA((4, 4)), pltpu.SemaphoreType.DMA((4, 4)),
         pltpu.SemaphoreType.DMA((4,)), pltpu.SemaphoreType.DMA((4,)),

time: 36.3 us -> 34.8 us (0.959)
  Pallas kernels: 35.5 us -> 34.1 us
    pallas_call x1, Pallas kernels: 33.8 us -> 32.4 us  [per_device(): pl.pallas_call(functools.partial(kernel, n_lat, n_lon), out_shape=(jax.Sh...]
where the time goes in v4:
time: 34.8 us; the launch traced here: 34.7 us
  Pallas kernels  34.1 us (98%)
  between operations  0.64 us (2%)
    pallas_call x1, Pallas kernels, per_device(): pl.pallas_call(functools.partial(kernel, n_lat, n_lon), out_shape=(jax.Sh...  32.4 us
    pallas_call x1, Pallas kernels, per_device(): pl.pallas_call(write_out, out_shape=(jax.ShapeDtypeStruct(block, BF), jax...  1.7 us

profile of v4, /device:TPU:1, one launch (start us, length us, event | category | flops | bytes accessed | tf_op | source)
XLA Modules:
  0.0 34.7 jit_solution(5465384845835663959)
XLA Ops:
  0.6 32.4 %shard_map.167 = (bf16[72,2,512]{2,1,0:T(2,128)(2,1)}, bf16[72,2,512]{2,1,0:T(2,128)(2,1)}) custom-call(bf16[72,2,512]{2,1,0:T(2,128)(2,1)} %bitcast.16, s32[6,2,12]{2,1,0:T(2,128)} %bitcast.18, f32[1,512]{1,0:T(1,128)} %bitcast.19, bf16[512,1536]{1,0:T(8,128)(2,1)} %project_one.1, bf16[512,512]{1,0:T(8,128)(2,1)} %output_one.1, ...), custom_call_target="tpu_custom_call" | custom-call | tf_op jit(solution)/shard_map/pallas_call | solution.py:415
  33.0 1.7 %shard_map.168 = (bf16[72,2,512]{2,1,0:T(2,128)(2,1)}, bf16[72,2,512]{2,1,0:T(2,128)(2,1)}) custom-call(bf16[72,2,512]{2,1,0:T(2,128)(2,1)} %get-tuple-element.6.first, bf16[72,2,512]{2,1,0:T(2,128)(2,1)} %get-tuple-element.7.second), custom_call_target="tpu_custom_call" | custom-call | tf_op jit(solution)/shard_map/pallas_call | solution.py:425

commit v5 on v4

--- a/solution.py
+++ b/solution.py
@@ -173,8 +173,8 @@
     x, ct, packed_one, packed_two, probs_one, probs_two, heads_one, heads_two, d_heads, d_packed,
     hat_one, hat_two, inv_one, inv_two, hidden, dh_keep, table_two, w1t, wo1t, w2t, wo2t, wupt,
     out_stage, grad_stage,
-    send, recv, lab_send, lab_recv,
-    load_sem, send_sem, recv_sem, lab_send_sem, lab_recv_sem, out_sem,
+    send, recv, first_send, first_recv,
+    load_sem, send_sem, recv_sem, out_sem,
 ):
     i = lax.axis_index("lat")
     j = lax.axis_index("lon")
@@ -186,16 +186,20 @@
         pl.semaphore_signal(barrier, inc=1, device_id=device, device_id_type=MESH)
 
     pairs = {
-        "tok": (tokens, tok), "g1": (gain_one, g1), "w1": (project_one, w1), "b1": (bias_one, b1),
-        "lab": (labels, lab), "tq": (to_quad, tq), "fq": (from_quad, fq),
-        "wo1": (output_one, wo1), "g2": (gain_two, g2), "cot": (cotangent, cot), "w2": (project_two, w2),
-        "wdn": (down_weight, wdn), "b2": (bias_two, b2),
-        "wo2": (output_two, wo2), "g3": (gain_three, g3), "wup": (up_weight, wup),
+        "tok": (tokens, tok), "g1": (gain_one, g1), "w1": (project_one, w1),
+        "tq": (to_quad, tq), "cot": (cotangent, cot), "lab": (labels, lab),
+        "b1": (bias_one, b1), "wo1": (output_one, wo1),
+        "wup": (up_weight, wup), "w2": (project_two, w2), "wo2": (output_two, wo2),
+        "fq": (from_quad, fq), "wdn": (down_weight, wdn), "b2": (bias_two, b2),
+        "g2": (gain_two, g2), "g3": (gain_three, g3),
     }
-    loads = {}
-    for at, (name, (source, target)) in enumerate(pairs.items()):
-        loads[name] = pltpu.make_async_copy(source, target, load_sem.at[at])
-        loads[name].start()
+    loads = {
+        name: pltpu.make_async_copy(source, target, load_sem.at[at])
+        for at, (name, (source, target)) in enumerate(pairs.items())
+    }
+    ordered = list(loads.values())
+    for load in ordered[:8]:
+        load.start()
 
     masks = head_masks()
 
@@ -225,6 +229,10 @@
             last = jnp.where(quarters[k], rest[:, LANES * k : LANES * (k + 1)], last)
         target[8] = last
 
+    def add(target, rows, q):
+        for a in range(3):
+            target[9 + a] = rows[SLOT * q + TILE * a : SLOT * q + TILE * (a + 1)]
+
     def unpack(source):
         rows = [
             jnp.concatenate([source[4 * a + k] for k in range(GROUPS)], axis=1) for a in range(2)
@@ -234,15 +242,20 @@
         rows.append(jnp.concatenate([jnp.where(m, last, zero) for m in quarters], axis=1))
         return jnp.concatenate(rows, axis=0)
 
-    def start(step, targets, value):
+    def start(step, targets, value, extra=None):
         rows = nn(tq[...], value).astype(BF)
         copies = []
         for q, device in targets.items():
-            pack(send.at[step, q], rows[SLOT * q : SLOT * (q + 1)])
+            if extra is None:
+                source, target = (send.at[step, q], recv.at[step, 3 - q])
+            else:
+                source, target = (first_send.at[q], first_recv.at[3 - q])
+                add(source, extra, q)
+            pack(source, rows[SLOT * q : SLOT * (q + 1)])
             copies.append(
                 pltpu.make_async_remote_copy(
-                    src_ref=send.at[step, q],
-                    dst_ref=recv.at[step, 3 - q],
+                    src_ref=source,
+                    dst_ref=target,
                     send_sem=send_sem.at[step, q],
                     recv_sem=recv_sem.at[step, q],
                     device_id=device,
@@ -251,13 +264,19 @@
             )
             copies[-1].start()
         stay = 0 if targets is owner_target else 3
-        pack(recv.at[step, 3 - stay], rows[SLOT * stay : SLOT * (stay + 1)])
+        if extra is None:
+            target = recv.at[step, 3 - stay]
+        else:
+            target = first_recv.at[3 - stay]
+            add(target, extra, stay)
+        pack(target, rows[SLOT * stay : SLOT * (stay + 1)])
         return copies
 
     def arrived(step, copies):
         for copy in copies:
             copy.wait_recv()
-        return nn(fq[...], jnp.concatenate([unpack(recv.at[step, q]) for q in range(4)], axis=0))
+        blocks = first_recv if step == 0 else recv.at[step]
+        return nn(fq[...], jnp.concatenate([unpack(blocks.at[q]) for q in range(4)], axis=0))
 
     loads["tok"].wait()
     to_rows(tok, x)
@@ -265,10 +284,8 @@
     hat, rs_one = norm_parts(x[...])
     hat_one[...] = hat
     normed = (hat * g1[...]).astype(BF)
-    loads["w1"].wait()
-    packed_one[...] = nn(normed, w1[...]).astype(BF)
-
-    for name in ("lab", "tq", "fq", "cot"):
+
+    for name in ("lab", "tq", "cot"):
         loads[name].wait()
     token = lax.broadcasted_iota(jnp.int32, (WT, WLON), 0)
     column = lax.broadcasted_iota(jnp.int32, (WT, WLON), 1)
@@ -285,25 +302,13 @@
         spare = jnp.logical_and(row >= SLOT * q + QUAD, row < SLOT * (q + 1))
         label_rows = jnp.where(spare, 0.0, label_rows)
     label_rows = label_rows.astype(BF)
-    lab_send[...] = label_rows
-    lab_recv[pl.ds(3 * SLOT, SLOT)] = label_rows[:SLOT]
     to_rows(cot, ct)
+    loads["w1"].wait()
+    packed_one[...] = nn(normed, w1[...]).astype(BF)
+    for load in ordered[8:]:
+        load.start()
     pl.semaphore_wait(barrier, len(around))
-    lab_copies = []
-    for q, device in owner_target.items():
-        lab_copies.append(
-            pltpu.make_async_remote_copy(
-                src_ref=lab_send.at[pl.ds(SLOT * q, SLOT)],
-                dst_ref=lab_recv.at[pl.ds(SLOT * (3 - q), SLOT)],
-                send_sem=lab_send_sem.at[q],
-                recv_sem=lab_recv_sem.at[q],
-                device_id=device,
-                device_id_type=MESH,
-            )
-        )
-        lab_copies[-1].start()
-    cot_copies = start(0, owner_target, ct[...].astype(BF))
-
+    cot_copies = start(0, owner_target, ct[...].astype(BF), label_rows)
     loads["b1"].wait()
 
     def weight_one(score, h):
@@ -318,12 +323,15 @@
     loads["wo1"].wait()
     mid_copies = start(1, owner_target, (x[...] + nn(heads_one[...], wo1[...])).astype(BF))
 
+    for name in ("wup", "w2", "wo2", "fq"):
+        loads[name].wait()
+    for weight, turned in ((wup, wupt), (w2, w2t), (wo2, wo2t)):
+        turned[...] = weight[...].T
     ct[...] = arrived(0, cot_copies)
     loads["wdn"].wait()
     dh_keep[...] = (0.5 * nt(ct[...].astype(BF), wdn[...])).astype(BF)
-    for copy in lab_copies:
-        copy.wait_recv()
-    label_here = nn(fq[...], lab_recv[...])
+    label_rows = [first_recv[q, 9 + a] for q in range(4) for a in range(3)]
+    label_here = nn(fq[...], jnp.concatenate(label_rows, axis=0))
     row = lax.broadcasted_iota(jnp.int32, (WT, LANES), 0)
     late_row = jnp.logical_or(
         jnp.logical_and(row >= PLANE // 2, row < PLANE), row >= PLANE + PLANE // 2
@@ -336,10 +344,8 @@
     loads["b2"].wait()
     for h in range(HEADS):
         table_two[h] = b2[h].astype(F32) * LOG2E + barred
-    for name in ("g2", "w2", "wo2", "g3", "wup"):
+    for name in ("g2", "g3"):
         loads[name].wait()
-    for weight, turned in ((wup, wupt), (w2, w2t), (wo2, wo2t), (w1, w1t), (wo1, wo1t)):
-        turned[...] = weight[...].T
 
     mid = arrived(1, mid_copies)
     hat, rs_two = norm_parts(mid)
@@ -359,6 +365,9 @@
     d_mid = d_late + norm_back(hat_two[...], rs_two, g2[...], dn)
     back_copies = start(2, window_target, d_mid.astype(BF))
     out_copies = start(3, window_target, (late + nn(hidden[...], wdn[...])).astype(BF))
+
+    for weight, turned in ((wo1, wo1t), (w1, w1t)):
+        turned[...] = weight[...].T
 
     d_mid = arrived(2, back_copies)
     d_heads[...] = nn(d_mid.astype(BF), wo1t[...]).astype(BF)
@@ -370,7 +379,7 @@
     to_cells(d_mid + norm_back(hat_one[...], rs_one, g1[...], dn), grad_stage)
     grad_copy = pltpu.make_async_copy(grad_stage, input_grad, out_sem.at[1])
     grad_copy.start()
-    for copy in lab_copies + cot_copies + mid_copies + back_copies + out_copies:
+    for copy in cot_copies + mid_copies + back_copies + out_copies:
         copy.wait_send()
     out_copy.wait()
     grad_copy.wait()
@@ -405,10 +414,10 @@
         vm((WT, FF), BF), vm((WT, FF), BF), vm((HEADS, WT, WT), F32),
         vm((3 * D, D), BF), vm((D, D), BF), vm((3 * D, D), BF), vm((D, D), BF), vm((FF, D), BF),
         vm(block, BF), vm(block, BF),
-        vm((4, 4, 9, TILE, LANES), BF), vm((4, 4, 9, TILE, LANES), BF), vm((ROWS, LANES), BF), vm((ROWS, LANES), BF),
+        vm((4, 4, 9, TILE, LANES), BF), vm((4, 4, 9, TILE, LANES), BF),
+        vm((4, 12, TILE, LANES), BF), vm((4, 12, TILE, LANES), BF),
         pltpu.SemaphoreType.DMA((len(operands),)),
         pltpu.SemaphoreType.DMA((4, 4)), pltpu.SemaphoreType.DMA((4, 4)),
-        pltpu.SemaphoreType.DMA((4,)), pltpu.SemaphoreType.DMA((4,)),
         pltpu.SemaphoreType.DMA((2,)),
     ]
     whole = pl.BlockSpec(memory_space=pl.ANY)

time: 34.8 us -> 32.7 us (0.940)
  Pallas kernels: 34.1 us -> 32 us
    pallas_call x1, Pallas kernels: 32.4 us -> 30.3 us  [per_device(): pl.pallas_call(functools.partial(kernel, n_lat, n_lon), out_shape=(jax.Sh...]
where the time goes in v5:
time: 32.7 us; the launch traced here: 32.6 us
  Pallas kernels  32 us (98%)
  between operations  0.64 us (2%)
    pallas_call x1, Pallas kernels, per_device(): pl.pallas_call(functools.partial(kernel, n_lat, n_lon), out_shape=(jax.Sh...  30.3 us
    pallas_call x1, Pallas kernels, per_device(): pl.pallas_call(write_out, out_shape=(jax.ShapeDtypeStruct(block, BF), jax...  1.7 us

profile of v5, /device:TPU:1, one launch (start us, length us, event | category | flops | bytes accessed | tf_op | source)
XLA Modules:
  0.0 32.6 jit_solution(8811704313140776842)
XLA Ops:
  0.6 30.3 %shard_map.167 = (bf16[72,2,512]{2,1,0:T(2,128)(2,1)}, bf16[72,2,512]{2,1,0:T(2,128)(2,1)}) custom-call(bf16[72,2,512]{2,1,0:T(2,128)(2,1)} %bitcast.16, s32[6,2,12]{2,1,0:T(2,128)} %bitcast.18, f32[1,512]{1,0:T(1,128)} %bitcast.19, bf16[512,1536]{1,0:T(8,128)(2,1)} %project_one.1, bf16[512,512]{1,0:T(8,128)(2,1)} %output_one.1, ...), custom_call_target="tpu_custom_call" | custom-call | tf_op jit(solution)/shard_map/pallas_call | solution.py:424
  30.9 1.7 %shard_map.168 = (bf16[72,2,512]{2,1,0:T(2,128)(2,1)}, bf16[72,2,512]{2,1,0:T(2,128)(2,1)}) custom-call(bf16[72,2,512]{2,1,0:T(2,128)(2,1)} %get-tuple-element.6.first, bf16[72,2,512]{2,1,0:T(2,128)(2,1)} %get-tuple-element.7.second), custom_call_target="tpu_custom_call" | custom-call | tf_op jit(solution)/shard_map/pallas_call | solution.py:434

commit v6 on v5

--- a/solution.py
+++ b/solution.py
@@ -172,9 +172,8 @@
     tok, lab, g1, w1, wo1, b1, g2, w2, wo2, b2, g3, wup, wdn, cot, tq, fq,
     x, ct, packed_one, packed_two, probs_one, probs_two, heads_one, heads_two, d_heads, d_packed,
     hat_one, hat_two, inv_one, inv_two, hidden, dh_keep, table_two, w1t, wo1t, w2t, wo2t, wupt,
-    out_stage, grad_stage,
     send, recv, first_send, first_recv,
-    load_sem, send_sem, recv_sem, out_sem,
+    load_sem, send_sem, recv_sem,
 ):
     i = lax.axis_index("lat")
     j = lax.axis_index("lon")
@@ -186,8 +185,8 @@
         pl.semaphore_signal(barrier, inc=1, device_id=device, device_id_type=MESH)
 
     pairs = {
-        "tok": (tokens, tok), "g1": (gain_one, g1), "w1": (project_one, w1),
-        "tq": (to_quad, tq), "cot": (cotangent, cot), "lab": (labels, lab),
+        "tok": (tokens, tok), "g1": (gain_one, g1), "lab": (labels, lab), "tq": (to_quad, tq),
+        "cot": (cotangent, cot), "w1": (project_one, w1),
         "b1": (bias_one, b1), "wo1": (output_one, wo1),
         "wup": (up_weight, wup), "w2": (project_two, w2), "wo2": (output_two, wo2),
         "fq": (from_quad, fq), "wdn": (down_weight, wdn), "b2": (bias_two, b2),
@@ -212,7 +211,7 @@
             target[:, level, :] = value[PLANE * level : PLANE * (level + 1)].astype(BF)
 
     owner_target = {3: (south, east), 1: (i, east), 2: (south, j)}
-    window_target = {0: (north, west), 2: (i, west), 1: (north, j)}
+    window_target = {1: (north, j), 0: (north, west), 2: (i, west)}
 
     quarter = lax.broadcasted_iota(jnp.int32, (TILE, LANES), 0)
     quarters = [
@@ -372,17 +371,11 @@
     d_mid = arrived(2, back_copies)
     d_heads[...] = nn(d_mid.astype(BF), wo1t[...]).astype(BF)
     attention_back(packed_one, probs_one, heads_one, inv_one, d_heads, d_packed, masks)
-    to_cells(arrived(3, out_copies), out_stage)
-    out_copy = pltpu.make_async_copy(out_stage, outputs, out_sem.at[0])
-    out_copy.start()
+    to_cells(arrived(3, out_copies), outputs)
     dn = nn(d_packed[...], w1t[...]).astype(BF).astype(F32)
-    to_cells(d_mid + norm_back(hat_one[...], rs_one, g1[...], dn), grad_stage)
-    grad_copy = pltpu.make_async_copy(grad_stage, input_grad, out_sem.at[1])
-    grad_copy.start()
+    to_cells(d_mid + norm_back(hat_one[...], rs_one, g1[...], dn), input_grad)
     for copy in cot_copies + mid_copies + back_copies + out_copies:
         copy.wait_send()
-    out_copy.wait()
-    grad_copy.wait()
 
 
 def write_out(first, second, first_out, second_out):
@@ -413,24 +406,23 @@
         vm((WT, D), F32), vm((WT, D), F32), vm((WT, D), F32), vm((WT, D), F32),
         vm((WT, FF), BF), vm((WT, FF), BF), vm((HEADS, WT, WT), F32),
         vm((3 * D, D), BF), vm((D, D), BF), vm((3 * D, D), BF), vm((D, D), BF), vm((FF, D), BF),
-        vm(block, BF), vm(block, BF),
         vm((4, 4, 9, TILE, LANES), BF), vm((4, 4, 9, TILE, LANES), BF),
         vm((4, 12, TILE, LANES), BF), vm((4, 12, TILE, LANES), BF),
         pltpu.SemaphoreType.DMA((len(operands),)),
         pltpu.SemaphoreType.DMA((4, 4)), pltpu.SemaphoreType.DMA((4, 4)),
-        pltpu.SemaphoreType.DMA((2,)),
     ]
     whole = pl.BlockSpec(memory_space=pl.ANY)
     results = pl.pallas_call(
         functools.partial(kernel, n_lat, n_lon),
-        out_shape=(jax.ShapeDtypeStruct(block, BF), jax.ShapeDtypeStruct(block, BF)),
+        out_shape=(pltpu.VMEM(block, BF), pltpu.VMEM(block, BF)),
         in_specs=[whole] * len(operands),
-        out_specs=(whole, whole),
+        out_specs=[pl.BlockSpec(memory_space=pltpu.VMEM)] * 2,
         scratch_shapes=scratch,
         compiler_params=pltpu.CompilerParams(
             collective_id=0, has_side_effects=True, vmem_limit_bytes=56 * 1024 * 1024
         ),
     )(*operands)
+    results = [pltpu.with_memory_space_constraint(a, pltpu.VMEM) for a in results]
     results = pl.pallas_call(
         write_out,
         out_shape=(jax.ShapeDtypeStruct(block, BF), jax.ShapeDtypeStruct(block, BF)),

time: 32.7 us -> 30.7 us (0.939)
  Pallas kernels: 32 us -> 30 us
    pallas_call x1, Pallas kernels: 30.3 us -> 29.3 us  [per_device(): pl.pallas_call(functools.partial(kernel, n_lat, n_lon), out_shape=(pltpu....]
    pallas_call x1, Pallas kernels: 1.7 us -> 0.73 us  [per_device(): pl.pallas_call(write_out, out_shape=(jax.ShapeDtypeStruct(block, BF), jax...]
where the time goes in v6:
time: 30.7 us; the launch traced here: 30.6 us
  Pallas kernels  30 us (98%)
  between operations  0.64 us (2%)
    pallas_call x1, Pallas kernels, per_device(): pl.pallas_call(functools.partial(kernel, n_lat, n_lon), out_shape=(pltpu....  29.3 us
    pallas_call x1, Pallas kernels, per_device(): pl.pallas_call(write_out, out_shape=(jax.ShapeDtypeStruct(block, BF), jax...  0.73 us

profile of v6, /device:TPU:1, one launch (start us, length us, event | category | flops | bytes accessed | tf_op | source)
XLA Modules:
  0.0 30.6 jit_solution(8592950022308026986)
XLA Ops:
  0.6 29.3 %shard_map.167 = (bf16[72,2,512]{2,1,0:T(2,128)(2,1)S(1)}, bf16[72,2,512]{2,1,0:T(2,128)(2,1)S(1)}) custom-call(bf16[72,2,512]{2,1,0:T(2,128)(2,1)} %bitcast.16, s32[6,2,12]{2,1,0:T(2,128)} %bitcast.18, f32[1,512]{1,0:T(1,128)} %bitcast.19, bf16[512,1536]{1,0:T(8,128)(2,1)} %project_one.1, bf16[512,512]{1,0:T(8,128)(2,1)} %output_one.1, ...), custom_call_target="tpu_custom_call" | custom-call | tf_op jit(solution)/shard_map/pallas_call | solution.py:415
  29.9 0.7 %shard_map.168 = (bf16[72,2,512]{2,1,0:T(2,128)(2,1)}, bf16[72,2,512]{2,1,0:T(2,128)(2,1)}) custom-call(bf16[72,2,512]{2,1,0:T(2,128)(2,1)S(1)} %get-tuple-element.6.first, bf16[72,2,512]{2,1,0:T(2,128)(2,1)S(1)} %get-tuple-element.7.second), custom_call_target="tpu_custom_call" | custom-call | tf_op jit(solution)/shard_map/pallas_call | solution.py:426

commit v7 on v6

--- a/solution.py
+++ b/solution.py
@@ -241,7 +241,7 @@
         rows.append(jnp.concatenate([jnp.where(m, last, zero) for m in quarters], axis=1))
         return jnp.concatenate(rows, axis=0)
 
-    def start(step, targets, value, extra=None):
+    def start(step, targets, value, extra=None, go=True):
         rows = nn(tq[...], value).astype(BF)
         copies = []
         for q, device in targets.items():
@@ -261,7 +261,8 @@
                     device_id_type=MESH,
                 )
             )
-            copies[-1].start()
+            if go:
+                copies[-1].start()
         stay = 0 if targets is owner_target else 3
         if extra is None:
             target = recv.at[step, 3 - stay]
@@ -302,12 +303,14 @@
         label_rows = jnp.where(spare, 0.0, label_rows)
     label_rows = label_rows.astype(BF)
     to_rows(cot, ct)
+    cot_copies = start(0, owner_target, ct[...].astype(BF), label_rows, go=False)
     loads["w1"].wait()
     packed_one[...] = nn(normed, w1[...]).astype(BF)
     for load in ordered[8:]:
         load.start()
     pl.semaphore_wait(barrier, len(around))
-    cot_copies = start(0, owner_target, ct[...].astype(BF), label_rows)
+    for copy in cot_copies:
+        copy.start()
     loads["b1"].wait()
 
     def weight_one(score, h):

time: 30.7 us -> 30.5 us (level)
  no operation moved by 1% of the time
where the time goes in v7:
time: 30.5 us; the launch traced here: 30.4 us
  Pallas kernels  29.7 us (97%)
  between operations  0.64 us (2%)
    pallas_call x1, Pallas kernels, per_device(): pl.pallas_call(functools.partial(kernel, n_lat, n_lon), out_shape=(pltpu....  29 us
    pallas_call x1, Pallas kernels, per_device(): pl.pallas_call(write_out, out_shape=(jax.ShapeDtypeStruct(block, BF), jax...  0.73 us

profile of v7, /device:TPU:1, one launch (start us, length us, event | category | flops | bytes accessed | tf_op | source)
XLA Modules:
  0.0 30.4 jit_solution(12648765946863169781)
XLA Ops:
  0.6 29.0 %shard_map.167 = (bf16[72,2,512]{2,1,0:T(2,128)(2,1)S(1)}, bf16[72,2,512]{2,1,0:T(2,128)(2,1)S(1)}) custom-call(bf16[72,2,512]{2,1,0:T(2,128)(2,1)} %bitcast.16, s32[6,2,12]{2,1,0:T(2,128)} %bitcast.18, f32[1,512]{1,0:T(1,128)} %bitcast.19, bf16[512,1536]{1,0:T(8,128)(2,1)} %project_one.1, bf16[512,512]{1,0:T(8,128)(2,1)} %output_one.1, ...), custom_call_target="tpu_custom_call" | custom-call | tf_op jit(solution)/shard_map/pallas_call | solution.py:418
  29.7 0.7 %shard_map.168 = (bf16[72,2,512]{2,1,0:T(2,128)(2,1)}, bf16[72,2,512]{2,1,0:T(2,128)(2,1)}) custom-call(bf16[72,2,512]{2,1,0:T(2,128)(2,1)S(1)} %get-tuple-element.6.first, bf16[72,2,512]{2,1,0:T(2,128)(2,1)S(1)} %get-tuple-element.7.second), custom_call_target="tpu_custom_call" | custom-call | tf_op jit(solution)/shard_map/pallas_call | solution.py:429

commit v8 on v7

--- a/solution.py
+++ b/solution.py
@@ -126,11 +126,9 @@
         left = jnp.concatenate([do, spread(less, masks)], axis=1)
         return do, nt(left, jnp.concatenate([v, jnp.ones_like(v)], axis=1))
 
-    ahead = [first(0), first(1)]
+    ahead = [first(g) for g in range(GROUPS)]
     for g in range(GROUPS):
         do, dp = ahead.pop(0)
-        if g + 2 < GROUPS:
-            ahead.append(first(g + 2))
         q, k, _ = group(packed, g)
         p = probs[pl.ds(WT * PER * g, WT * PER), :]
         dv = tn(p, do)

time: 30.5 us -> 30.5 us (level)
  no operation moved by 1% of the time
where the time goes in v8:
time: 30.5 us; the launch traced here: 30.4 us
  Pallas kernels  29.8 us (98%)
  between operations  0.64 us (2%)
    pallas_call x1, Pallas kernels, per_device(): pl.pallas_call(functools.partial(kernel, n_lat, n_lon), out_shape=(pltpu....  29 us
    pallas_call x1, Pallas kernels, per_device(): pl.pallas_call(write_out, out_shape=(jax.ShapeDtypeStruct(block, BF), jax...  0.73 us

profile of v8, /device:TPU:1, one launch (start us, length us, event | category | flops | bytes accessed | tf_op | source)
XLA Modules:
  0.0 30.4 jit_solution(2900924223128995512)
XLA Ops:
  0.6 29.0 %shard_map.167 = (bf16[72,2,512]{2,1,0:T(2,128)(2,1)S(1)}, bf16[72,2,512]{2,1,0:T(2,128)(2,1)S(1)}) custom-call(bf16[72,2,512]{2,1,0:T(2,128)(2,1)} %bitcast.16, s32[6,2,12]{2,1,0:T(2,128)} %bitcast.18, f32[1,512]{1,0:T(1,128)} %bitcast.19, bf16[512,1536]{1,0:T(8,128)(2,1)} %project_one.1, bf16[512,512]{1,0:T(8,128)(2,1)} %output_one.1, ...), custom_call_target="tpu_custom_call" | custom-call | tf_op jit(solution)/shard_map/pallas_call | solution.py:416
  29.7 0.7 %shard_map.168 = (bf16[72,2,512]{2,1,0:T(2,128)(2,1)}, bf16[72,2,512]{2,1,0:T(2,128)(2,1)}) custom-call(bf16[72,2,512]{2,1,0:T(2,128)(2,1)S(1)} %get-tuple-element.6.first, bf16[72,2,512]{2,1,0:T(2,128)(2,1)S(1)} %get-tuple-element.7.second), custom_call_target="tpu_custom_call" | custom-call | tf_op jit(solution)/shard_map/pallas_call | solution.py:427
